TPU v7x, 32 devices: a whole 2x2x4 slice. The times are simulated.
32 devices in a mesh: shards: 2 (over x), context: 4 (over y, core), tensor: 4 (over z).
Axes of the slice: x: 2, y: 2, z: 4, core: 2. Of those that a mesh axis runs over, the one named last changes fastest.
Arguments:
- hidden_in: bfloat16 [2, 1024, 1024], P('shards', 'context'), may hold values from -6 to 6
- positions: int32 [2, 1024], P('shards'), may hold values from 0 to 1023, each once within a row
- routes: int32 [2, 1024, 8], P('shards', 'context'), may hold values from 0 to 31, all different within a row; in each aligned block of 256 rows (0 to 255, 256 to 511, ..., all dimensions but the last counted through in order) at most 96 rows name the same one
- out_grad: bfloat16 [2, 1024, 1024], P('shards', 'context'), may hold values from -6 to 6
- attn_gain: bfloat16 [1024], P(('shards', 'context')), may hold values from 0.5 to 1.5
- query_weight: bfloat16 [1024, 1024], P(('shards', 'context'), 'tensor'), may hold values from -0.75 to 0.75
- key_matrix: bfloat16 [1024, 512], P(('shards', 'context'), 'tensor'), may hold values from -0.75 to 0.75
- value_matrix: bfloat16 [1024, 512], P(('shards', 'context'), 'tensor'), may hold values from -0.1875 to 0.1875
- out_weight: bfloat16 [1024, 1024], P(('shards', 'context'), 'tensor'), may hold values from -3 to 3
- moe_gain: bfloat16 [1024], P(('shards', 'context')), may hold values from 0.5 to 1.5
- router_weight: bfloat16 [1024, 32], P(('shards', 'context')), may hold values from -0.09375 to 0.09375
- gate_weight: bfloat16 [32, 1024, 512], P('context', 'shards', 'tensor'), may hold values from -0.1875 to 0.1875
- up_weight: bfloat16 [32, 1024, 512], P('context', 'shards', 'tensor'), may hold values from -0.1875 to 0.1875
- down_weight: bfloat16 [32, 1024, 512], P('context', 'shards', 'tensor'), may hold values from -6 to 6
Outputs:
- block_out: bfloat16 [2, 1024, 1024], P('shards', 'context')
- in_grad: float32 [2, 1024, 1024], P('shards', 'context')
- attn_gain_grad: float32 [1024], P(('shards', 'context'))
- query_weight_grad: float32 [1024, 1024], P(('shards', 'context'), 'tensor')
- key_weight_grad: float32 [1024, 512], P(('shards', 'context'), 'tensor')
- value_weight_grad: float32 [1024, 512], P(('shards', 'context'), 'tensor')
- out_weight_grad: float32 [1024, 1024], P(('shards', 'context'), 'tensor')
- moe_gain_grad: float32 [1024], P(('shards', 'context'))
- router_grad: float32 [1024, 32], P(('shards', 'context'))
- gate_weight_grad: float32 [32, 1024, 512], P('context', 'shards', 'tensor')
- up_weight_grad: float32 [32, 1024, 512], P('context', 'shards', 'tensor')
- down_weight_grad: float32 [32, 1024, 512], P('context', 'shards', 'tensor')
Inputs may be any that keep to these rules, and one draw needn't show every extreme that they name: `positions`: each sequence's row holds every position once. `routes`: each token names 8 different experts; among the tokens of one device (aligned blocks of 256 tokens) no expert is named more than 96 times, and in every draw some block names some expert exactly 96 times.
All inputs are finite; a program needn't handle non-finite values.
Results may differ from a plain program's by a relative error of at most 0.02.
Values may be sent and summed in bfloat16 or wider, within the bound.
No kernel may reach another device: no remote copies, remote signals or barrier semaphores. Data moves between devices by JAX's collectives and lax.ppermute only.
A program may use at most 128 MiB of HBM per device.

v0:
```python
import functools

import jax
import jax.numpy as jnp
from jax import lax
from jax.experimental import pallas as pl
from jax.experimental.pallas import tpu as pltpu
from jax.sharding import PartitionSpec as P

HEAD_SIZE = 64
NORM_EPS = 1e-06
ATTN_MULT = 0.015625
RESID_MULT = 0.22
ROPE_BASE = 10000.0
F32 = jnp.float32
BF16 = jnp.bfloat16
VMEM_BYTES = 56 * 1024 * 1024
PART_ROWS = 1024
MICROSECONDS = {
    "project": 3,
    "assemble": 3,
    "middle": 4,
    "fold": 2.5,
    "middle_back": 4.5,
    "project_back": 3,
    "weights_back": 3,
    "attend": 4,
    "attend_back": 6,
    "experts": 12,
    "grads": 12,
    "outputs": 9,
}
LANES = 128


def swap(x, axis, bit):
    devices = lax.axis_size(axis)
    return lax.ppermute(x, axis, [(i, i ^ bit) for i in range(devices)])


def turn(x, k):
    return swap(x, "tensor", k)


def stepped():
    return lax.axis_size("context") == 4 and lax.axis_size("shards") == 2


def after(x, *others):
    return lax.optimization_barrier((x,) + others)[0]


def gather_context(x):
    if not stepped():
        return [lax.all_gather(x, "context", axis=0, tiled=True)]
    across = swap(x, "context", 2)
    return [x, swap(x, "context", 1), across, swap(across, "context", 1)]


def swap_tensor(x, bit):
    return swap(x, "tensor", bit)


def gather_owners(x):
    if not stepped():
        return [lax.all_gather(x, ("shards", "context"))]
    far = []
    for m in (2, 4, 6):
        far.append(lax.ppermute(x, ("shards", "context"), [(i, i ^ m) for i in range(8)]))
    near = swap(x, "context", 1)
    odd = swap(jnp.concatenate(far, axis=0), "context", 1)
    size = x.shape[0]
    return [x] + far + [near] + [odd[i * size : (i + 1) * size] for i in range(3)]


OWNER_ORDER = (0, 4, 2, 6, 1, 5, 3, 7)


def scatter_owners(keep, send, travel):
    size = keep.shape[0] // 4
    total = keep.astype(F32) + swap(send.astype(travel), "context", 1).astype(F32)
    far = swap(total[2 * size :].astype(travel), "context", 2).astype(F32)
    total = total[: 2 * size] + far
    return total, total[:size] + swap(total[size:].astype(travel), "shards", 1).astype(F32)


def butterfly(x):
    bit = 1
    while bit < lax.axis_size("tensor"):
        x = x + lax.ppermute(x, "tensor", [(i, i ^ bit) for i in range(lax.axis_size("tensor"))])
        bit *= 2
    return x


def xor_blocks(pieces, index):
    pieces, bit = list(pieces), 1
    while bit < len(pieces):
        flag = (index & bit) != 0
        pieces = [jnp.where(flag, pieces[i ^ bit], pieces[i]) for i in range(len(pieces))]
        bit *= 2
    return pieces


def columns_of(x, count):
    size = x.shape[1] // count
    return [x[:, i * size : (i + 1) * size] for i in range(count)]


def cut(x, index, size):
    return lax.dynamic_slice_in_dim(x, index * size, size, axis=0)


def gather_tensor(x):
    devices, me = lax.axis_size("tensor"), lax.axis_index("tensor")
    size = x.shape[0]
    whole = jnp.zeros((size * devices,) + x.shape[1:], x.dtype)
    for k in range(devices):
        piece = turn(x, k) if k else x
        whole = lax.dynamic_update_slice_in_dim(whole, piece, (me ^ k) * size, axis=0)
    return whole


def nn(a, b):
    return lax.dot_general(a, b, (((1,), (0,)), ((), ())), preferred_element_type=F32)


def tn(a, b):
    return lax.dot_general(a, b, (((0,), (0,)), ((), ())), preferred_element_type=F32)


def nt(a, b):
    return lax.dot_general(a, b, (((1,), (1,)), ((), ())), preferred_element_type=F32)


def vmem():
    return pl.BlockSpec(memory_space=pltpu.VMEM)


def rotate(x, cosine, sine):
    lanes = x.shape[1]
    times = lanes // cosine.shape[1]
    lane = lax.broadcasted_iota(jnp.int32, x.shape, 1)
    half = HEAD_SIZE // 2
    partner = jnp.where(
        lane % HEAD_SIZE < half, pltpu.roll(x, lanes - half, 1), pltpu.roll(x, half, 1)
    )
    return x * jnp.concatenate([cosine] * times, 1) + partner * jnp.concatenate([sine] * times, 1)


def cost(name):
    flops = int(MICROSECONDS[name] * 1.15e9)
    return pl.CostEstimate(flops=flops, transcendentals=0, bytes_accessed=0)


def call(kernel, out_shape, operands, name, smem=(), **more):
    specs = [pl.BlockSpec(memory_space=pltpu.SMEM)] * len(smem) + [vmem()] * len(operands)
    return pl.pallas_call(
        kernel,
        out_shape=tuple(out_shape),
        in_specs=specs,
        out_specs=(vmem(),) * len(out_shape),
        compiler_params=pltpu.CompilerParams(vmem_limit_bytes=VMEM_BYTES),
        cost_estimate=cost(name),
        name=name,
        **more,
    )(*smem, *operands)


def shape(dims, dtype):
    return jax.ShapeDtypeStruct(tuple(dims), dtype)


def project_kernel(wide, narrow, chunk, hid_ref, gain_ref, cos_ref, sin_ref, *refs):
    *pieces, norm_ref, q_ref, kv_ref, w_ref = refs
    for i, piece in enumerate(pieces):
        w_ref[i * chunk : (i + 1) * chunk] = piece[:chunk, : w_ref.shape[1]]
    hid = hid_ref[...].astype(F32)
    scale = lax.rsqrt(jnp.mean(hid * hid, axis=1, keepdims=True) + NORM_EPS)
    normed = (hid * scale * gain_ref[...]).astype(BF16)
    norm_ref[...] = normed
    lin = nn(normed, w_ref[...])
    turned = rotate(lin[:, : wide + narrow], cos_ref[...], sin_ref[...]).astype(BF16)
    q_ref[...] = turned[:, :wide] * ATTN_MULT
    kv_ref[:, :narrow] = turned[:, wide:]
    kv_ref[:, narrow:] = lin[:, wide + narrow :].astype(BF16)


def project(hidden, gain, pieces, cosine, sine, wide, narrow, chunk):
    rows, width = hidden.shape
    return call(
        functools.partial(project_kernel, wide, narrow, chunk),
        (
            shape((rows, width), BF16),
            shape((rows, wide), BF16),
            shape((rows, 2 * narrow), BF16),
            shape((width, wide + 2 * narrow), BF16),
        ),
        (hidden, gain, cosine, sine, *pieces),
        "project",
    )


def assemble_kernel(order, chunk, place_ref, even_ref, odd_ref, out_ref):
    wide = even_ref.shape[1]
    size = len(order) // 2 * chunk
    for k in range(even_ref.shape[0] // size):
        for at, r in enumerate(order):
            start = k * size + at % (len(order) // 2) * chunk
            rows = pl.ds(pl.multiple_of((place_ref[3] ^ r) * chunk, chunk), chunk)
            source = (even_ref, odd_ref)[r % 2]
            out_ref[rows, k * wide : (k + 1) * wide] = source[start : start + chunk]


def middle_kernel(hid_ref, gain_ref, w_ref, *refs):
    *att_refs, mid_ref, norm_ref = refs
    attended = jnp.concatenate([r[...] for r in att_refs], axis=1)
    middle = hid_ref[...].astype(F32) + RESID_MULT * nt(attended, w_ref[...])
    scale = lax.rsqrt(jnp.mean(middle * middle, axis=1, keepdims=True) + NORM_EPS)
    mid_ref[...] = middle
    norm_ref[...] = (middle * scale * gain_ref[...]).astype(BF16)


def split_lanes(x):
    high = x.astype(BF16)
    low = (x - high.astype(F32)).astype(BF16).astype(F32)
    return (high.astype(F32) + pltpu.roll(low, LANES // 2, 1)).astype(BF16)


def join_lanes(x):
    lane = lax.broadcasted_iota(jnp.int32, x.shape, 1)
    return jnp.where(lane < LANES // 2, x + pltpu.roll(x, LANES // 2, 1), 0.0)


def fold_kernel(width, quarters, terms, place_ref, *refs):
    total = refs[0][...].astype(F32)
    for ref in refs[1:terms]:
        total = total + ref[...].astype(F32)
    if not quarters:
        ref = refs[terms]
        ref[:, :width] = total[:, :width].astype(BF16)
        if total.shape[1] > width:
            ref[:, width:] = split_lanes(join_lanes(total[:, width:]))
        return
    own_ref, *send_refs, total_ref = refs[terms:]
    if total.shape[1] > width:
        total = jnp.concatenate([total[:, :width], join_lanes(total[:, width:])], axis=1)
    total_ref[...] = total
    size = own_ref.shape[0]

    def part(index):
        index = place_ref[4] ^ index
        return total_ref[pl.ds(pl.multiple_of(index * size, size), size)]

    own_ref[...] = part(0)
    for k, ref in enumerate(send_refs, 1):
        found = part(k)
        ref[:, :width] = found[:, :width].astype(BF16)
        if found.shape[1] > width:
            ref[:, width:] = split_lanes(found[:, width:])


def fold(terms, place, width, quarters):
    rows, lanes = terms[0].shape
    size = rows // max(quarters, 1)
    outs = [shape((size, lanes), BF16)]
    if quarters:
        outs = [shape((size, lanes), F32)] + outs * (quarters - 1)
    return call(
        functools.partial(fold_kernel, width, quarters, len(terms)),
        outs,
        terms,
        "fold",
        smem=(place,),
        scratch_shapes=[pltpu.VMEM((rows, lanes), F32)] if quarters else [],
    )


def middle_back_kernel(width, _place_ref, mid_ref, norm_ref, gain_ref, grad_ref, gates_ref, router_ref, w_ref, *refs):
    outs = (len(refs) - 4) // 2
    parts, refs = refs[:outs], refs[outs:]
    dmid_ref, dattn_ref, dgain_ref, drouter_ref = refs[:4]
    total = parts[0][...]
    for part in parts[1:]:
        total = total + part[...].astype(F32)
    gates, d_gates = gates_ref[...], join_lanes(total[:, width:])
    d_picked = gates * (d_gates - jnp.sum(gates * d_gates, axis=1, keepdims=True))
    d_logits = d_picked.astype(BF16)
    drouter_ref[...] = tn(norm_ref[...], d_logits)
    d_normed = total[:, :width] + nt(d_logits, router_ref[...])
    d_rows, d_gain = rms_back(mid_ref[...], gain_ref[...], d_normed)
    d_middle = grad_ref[...].astype(F32) + d_rows
    d_attn = (RESID_MULT * d_middle).astype(BF16)
    dmid_ref[...], dattn_ref[...], dgain_ref[...] = d_middle, d_attn, d_gain
    d_attended = nn(d_attn, w_ref[...]).astype(BF16)
    wide = d_attended.shape[1] // outs
    for k, ref in enumerate(refs[4:]):
        ref[:, :wide] = d_attended[:, k * wide : (k + 1) * wide]
        if k:
            ref[:, wide:] = d_attn


def project_back_kernel(narrow, place_ref, dq_ref, keep_ref, came_ref, cos_ref, sin_ref, w_ref, hid_ref, *refs):
    own_ref, *send_refs, dlin_ref, dgain_ref, total_ref = refs
    d_kv = keep_ref[...].astype(F32) + came_ref[...].astype(F32)
    d_key = rotate(d_kv[:, :narrow], cos_ref[...], -sin_ref[...])
    d_lin = jnp.concatenate(
        [dq_ref[...], d_key.astype(BF16), d_kv[:, narrow:].astype(BF16)], axis=1
    )
    dlin_ref[...] = d_lin
    d_normed = nt(d_lin, w_ref[...])
    total_ref[...] = d_normed
    hid = hid_ref[...].astype(F32)
    scale = lax.rsqrt(jnp.mean(hid * hid, axis=1, keepdims=True) + NORM_EPS)
    dgain_ref[...] = jnp.sum(d_normed * hid * scale, axis=0, keepdims=True)
    size, quarters = own_ref.shape[0], 1 + len(send_refs)

    def part(k):
        index = place_ref[4] ^ k
        return total_ref[pl.ds(pl.multiple_of(index * size, size), size)]

    own_ref[...] = part(0)
    for k, ref in enumerate(send_refs, 1):
        ref[...] = part(k).astype(BF16)


def weights_back_kernel(order, chunk, place_ref, norm_ref, dlin_ref, att_ref, *refs):
    lin = tn(norm_ref[...], dlin_ref[...]).astype(BF16)
    *dattn_refs, keep_ref, send_ref, rows_ref, scratch_ref = refs
    size = dattn_refs[0].shape[0]
    for k, ref in enumerate(dattn_refs):
        columns = slice(ref.shape[1] - rows_ref.shape[1], None)
        rows_ref[pl.ds(pl.multiple_of((place_ref[4] ^ k) * size, size), size)] = ref[:, columns]
    scratch_ref[...] = tn(rows_ref[...], att_ref[...])
    split = lin.shape[1]
    for at, r in enumerate(order):
        ref = (keep_ref, send_ref)[r % 2]
        start = at % (len(order) // 2) * chunk
        rows = pl.ds(pl.multiple_of((place_ref[3] ^ r) * chunk, chunk), chunk)
        ref[start : start + chunk, :split] = lin[r * chunk : (r + 1) * chunk]
        ref[start : start + chunk, split:] = scratch_ref[rows].astype(BF16)


def whole_of(refs):
    return jnp.concatenate([r[...] for r in refs], axis=0) if len(refs) > 1 else refs[0][...]


def attend_kernel(heads, group, q_ref, own_ref, all_ref, *refs):
    *kv_refs, out_ref, lse_ref = refs
    kv = whole_of(kv_refs)
    narrow = kv.shape[1] // 2
    bias = jnp.where(all_ref[...] <= own_ref[...], 0.0, -1e30)
    for h in range(heads):
        at, kv_at = h * HEAD_SIZE, (h // group) * HEAD_SIZE
        key = kv[:, kv_at : kv_at + HEAD_SIZE]
        value = kv[:, narrow + kv_at : narrow + kv_at + HEAD_SIZE]
        scores = nt(q_ref[:, at : at + HEAD_SIZE], key) + bias
        top = jnp.max(scores, axis=1, keepdims=True)
        weights = jnp.exp(scores - top)
        total = jnp.sum(weights, axis=1, keepdims=True)
        out = nn(weights.astype(BF16), value) / total
        out_ref[:, at : at + HEAD_SIZE] = out.astype(BF16)
        lse_ref[:, h : h + 1] = top + jnp.log(total)


def attend(query, kv, own_places, all_places, heads, group):
    return call(
        functools.partial(attend_kernel, heads, group),
        (shape(query.shape, BF16), shape((query.shape[0], heads), F32)),
        (query, own_places, all_places, *kv),
        "attend",
    )


def attend_back_kernel(
    heads, group, quarters, blocks, place_ref, q_ref, own_ref, all_ref, lse_ref, cos_ref, sin_ref, *refs
):
    grads, refs = refs[:quarters], refs[quarters:]
    *kv_refs, dq_ref, keep_ref, send_ref, grad_ref = refs
    size = grads[0].shape[0]
    for k, ref in enumerate(grads):
        index = place_ref[4] ^ k
        grad_ref[pl.ds(pl.multiple_of(index * size, size), size)] = ref[:, : grad_ref.shape[1]]
    kv = whole_of(kv_refs)
    narrow = kv.shape[1] // 2
    bias = jnp.where(all_ref[...] <= own_ref[...], 0.0, -1e30)
    d_queries, d_keys, d_values = [], [], []
    for pair in range(heads // group):
        kv_at = pair * HEAD_SIZE
        key = kv[:, kv_at : kv_at + HEAD_SIZE]
        value = kv[:, narrow + kv_at : narrow + kv_at + HEAD_SIZE]
        d_key, d_value = 0.0, 0.0
        for h in range(pair * group, (pair + 1) * group):
            at = h * HEAD_SIZE
            query, grad = q_ref[:, at : at + HEAD_SIZE], grad_ref[:, at : at + HEAD_SIZE]
            probs = jnp.exp(nt(query, key) + bias - lse_ref[:, h : h + 1])
            d_probs = nt(grad, value)
            delta = jnp.sum(probs * d_probs, axis=1, keepdims=True)
            d_scores = (probs * (d_probs - delta)).astype(BF16)
            d_queries.append(nn(d_scores, key) * ATTN_MULT)
            d_key = d_key + tn(d_scores, query)
            d_value = d_value + tn(probs.astype(BF16), grad)
        d_keys.append(d_key)
        d_values.append(d_value)
    d_kv = jnp.concatenate(d_keys + d_values, axis=1).astype(BF16)
    rows = d_kv.shape[0] // blocks
    for m in range(blocks):
        ref = (keep_ref, send_ref)[m % 2]
        ref[m // 2 * rows : (m // 2 + 1) * rows] = d_kv[m * rows : (m + 1) * rows]
    d_query = jnp.concatenate(d_queries, axis=1)
    dq_ref[...] = rotate(d_query, cos_ref[...], -sin_ref[...]).astype(BF16)


def attend_back(blocks, query, kv, own_places, all_places, lse, grads, place, cosine, sine, heads, group):
    return call(
        functools.partial(attend_back_kernel, heads, group, len(grads), blocks),
        (shape(query.shape, BF16),)
        + (shape((sum(b.shape[0] for b in kv) // 2, kv[0].shape[1]), BF16),) * 2,
        (query, own_places, all_places, lse, cosine, sine, *grads, *kv),
        "attend_back",
        smem=(place,),
        scratch_shapes=[pltpu.VMEM(query.shape, BF16)],
    )


def gate_columns(gates, base, pair, units):
    lane = lax.broadcasted_iota(jnp.int32, gates.shape, 1)
    columns = [
        jnp.sum(jnp.where(lane == base + i, gates, 0.0), axis=1, keepdims=True) for i in range(pair)
    ]
    return jnp.concatenate(
        [jnp.broadcast_to(column, (gates.shape[0], units)) for column in columns], axis=1
    )


def whole_weight(first, own_ref, other_refs):
    pair = own_ref.shape[0]
    own = jnp.concatenate([own_ref[i] for i in range(pair)], axis=1)
    if not other_refs:
        return own
    other = jnp.concatenate([other_refs[0][i] for i in range(pair)], axis=1)
    for at, ref in enumerate(other_refs[1:], 1):
        here = jnp.concatenate([ref[i] for i in range(pair)], axis=1)
        other = jnp.where(pl.program_id(0) == at, here, other)
    return jnp.concatenate([jnp.where(first, own, other), jnp.where(first, other, own)], axis=0)


def experts_kernel(blocks, sources, counts, width, place_ref, router_ref, *refs):
    x_refs, g_refs, refs = refs[:sources], refs[sources : 2 * sources], refs[2 * sources :]
    (wg0_ref, wu0_ref, wd0_ref), refs = refs[:3], refs[3:]
    wg1_refs, refs = refs[: counts[0]], refs[counts[0] :]
    wu1_refs, refs = refs[: counts[1]], refs[counts[1] :]
    wd1_refs, refs = refs[: counts[2]], refs[counts[2] :]
    keep_ref, send_ref, own_ref, h_ref, dg_ref, du_ref, *refs = refs
    x_ref, grad_ref, gates_ref, din_acc, dgates_acc = refs
    step, steps = pl.program_id(0), pl.num_programs(0)
    pair, _, units = wg0_ref.shape
    first = place_ref[0] == 0
    base = place_ref[1] + step * pair
    rows = x_ref.shape[0] // blocks

    @pl.when(step == 0)
    def _():
        rows_in = whole_of(x_refs)
        x_ref[...] = rows_in
        grad_ref[...] = whole_of(g_refs)
        mask = grad_ref[:, width:].astype(F32)
        logits = jnp.where(mask > 0, nn(rows_in, router_ref[...]), -1e30)
        gates = mask * jnp.exp(logits - jnp.max(logits, axis=1, keepdims=True))
        gates = gates / jnp.sum(gates, axis=1, keepdims=True)
        gates_ref[...] = gates
        own_ref[...] = gates

    rows_in, rows_grad, gates = x_ref[...], grad_ref[:, :width], gates_ref[...]
    w_gate = whole_weight(first, wg0_ref, wg1_refs)
    w_up = whole_weight(first, wu0_ref, wu1_refs)
    w_down = whole_weight(first, wd0_ref, wd1_refs)
    wide = gate_columns(gates, base, pair, units)
    gate_pre, up_pre = nn(rows_in, w_gate), nn(rows_in, w_up)
    sigma = 0.5 * jnp.tanh(0.5 * gate_pre) + 0.5
    silu_gate = gate_pre * sigma
    active = silu_gate * up_pre
    h_ref[...] = (wide * active).astype(BF16)
    raw = nn(rows_grad, w_down)
    product = raw * active
    lane = lax.broadcasted_iota(jnp.int32, gates.shape, 1)
    d_gates = jnp.zeros_like(gates)
    for i in range(pair):
        column = RESID_MULT * jnp.sum(product[:, i * units : (i + 1) * units], axis=1, keepdims=True)
        d_gates = jnp.where(lane == base + i, column, d_gates)
    d_active = (RESID_MULT * wide) * raw
    d_gate_pre = (d_active * up_pre * sigma * (1.0 + gate_pre * (1.0 - sigma))).astype(BF16)
    d_up_pre = (d_active * silu_gate).astype(BF16)
    dg_ref[...], du_ref[...] = d_gate_pre, d_up_pre
    d_in = nt(d_gate_pre, w_gate) + nt(d_up_pre, w_up)

    @pl.when(step == 0)
    def _():
        din_acc[...] = d_in
        dgates_acc[...] = d_gates

    @pl.when(step > 0)
    def _():
        din_acc[...] += d_in
        dgates_acc[...] += d_gates

    @pl.when(step == steps - 1)
    def _():
        for m in range(blocks):
            ref = (keep_ref, send_ref)[m % 2]
            to, at = slice(m // 2 * rows, (m // 2 + 1) * rows), slice(m * rows, (m + 1) * rows)
            ref[to, :width] = din_acc[at].astype(BF16)
            ref[to, width:] = split_lanes(dgates_acc[at])


def held(a):
    return pl.BlockSpec(a.shape, lambda i: (0,) * len(a.shape))


def run_experts(blocks, chunks, x_blocks, g_blocks, router, place, weights, others):
    tokens, lanes = sum(b.shape[0] for b in x_blocks), g_blocks[0].shape[1]
    width = x_blocks[0].shape[1]
    count, _, units = weights[0].shape
    pair = count // chunks
    moving = lambda w: pl.BlockSpec((pair, w.shape[1], units), lambda i: (i, 0, 0))
    column = pl.BlockSpec((tokens, pair * units), lambda i: (0, i))
    outs = (
        [shape((tokens // 2, lanes), BF16)] * 2
        + [shape((tokens, LANES), F32)]
        + [shape((tokens, count * units), BF16)] * 3
    )
    flat = sum(others, [])
    return pl.pallas_call(
        functools.partial(experts_kernel, blocks, len(x_blocks), [len(o) for o in others], width),
        grid=(chunks,),
        out_shape=tuple(outs),
        in_specs=[pl.BlockSpec(memory_space=pltpu.SMEM), held(router)]
        + [held(b) for b in x_blocks + g_blocks]
        + [moving(w) for w in weights]
        + [held(o) for o in flat],
        out_specs=tuple(held(o) for o in outs[:3]) + (column,) * 3,
        scratch_shapes=[
            pltpu.VMEM((tokens, width), BF16),
            pltpu.VMEM((tokens, lanes), BF16),
            pltpu.VMEM((tokens, LANES), F32),
            pltpu.VMEM((tokens, width), F32),
            pltpu.VMEM((tokens, LANES), F32),
        ],
        compiler_params=pltpu.CompilerParams(vmem_limit_bytes=VMEM_BYTES),
        cost_estimate=cost("experts"),
        name="experts",
    )(place, router, *x_blocks, *g_blocks, *weights, *flat)


def grads_kernel(sources, parts, width, place_ref, *refs):
    x_refs, g_refs, refs = refs[:sources], refs[sources : 2 * sources], refs[2 * sources :]
    h_refs, dg_refs, du_refs = (refs[i * parts : (i + 1) * parts] for i in range(3))
    grad_refs = refs[3 * parts :]
    pair, half, units = grad_refs[0].shape
    first = place_ref[0] == 0

    def halves(grad, own_ref, other_ref):
        own = jnp.where(first, grad[:half], grad[half:]).astype(BF16)
        other = jnp.where(first, grad[half:], grad[:half]).astype(BF16)
        for i in range(pair):
            own_ref[i] = own[:, i * units : (i + 1) * units]
            other_ref[i] = other[:, i * units : (i + 1) * units]

    rows_in, rows_grad = whole_of(x_refs), whole_of(g_refs)[:, :width]
    halves(RESID_MULT * tn(rows_grad, whole_of(h_refs)), grad_refs[4], grad_refs[5])
    halves(tn(rows_in, whole_of(dg_refs)), grad_refs[0], grad_refs[1])
    halves(tn(rows_in, whole_of(du_refs)), grad_refs[2], grad_refs[3])


def run_grads(x_blocks, g_blocks, place, hidden, d_gate, d_up, dims, chunks):
    parts, tokens = len(hidden), sum(b.shape[0] for b in x_blocks)
    count, half, units = dims
    pair = count // chunks
    width = x_blocks[0].shape[1]
    moving = pl.BlockSpec((pair, half, units), lambda i: (i, 0, 0))
    column = pl.BlockSpec((tokens // parts, pair * units), lambda i: (0, i))
    return pl.pallas_call(
        functools.partial(grads_kernel, len(x_blocks), parts, width),
        grid=(chunks,),
        out_shape=(shape(dims, BF16),) * 6,
        in_specs=[pl.BlockSpec(memory_space=pltpu.SMEM)]
        + [held(b) for b in x_blocks + g_blocks]
        + [column] * (3 * parts),
        out_specs=(moving,) * 6,
        compiler_params=pltpu.CompilerParams(vmem_limit_bytes=VMEM_BYTES),
        cost_estimate=cost("grads"),
        name="grads",
    )(place, *x_blocks, *g_blocks, *hidden, *d_gate, *d_up)


def outputs_kernel(blocks, parts, chunks, place_ref, wd0_ref, *refs):
    h_refs, refs = refs[:parts], refs[parts:]
    wd1_refs, out_refs, out_acc = refs[:chunks], refs[chunks:-1], refs[-1]
    step, steps = pl.program_id(0), pl.num_programs(0)
    out = nt(whole_of(h_refs), whole_weight(place_ref[0] == 0, wd0_ref, wd1_refs))

    @pl.when(step == 0)
    def _():
        out_acc[...] = out

    @pl.when(step > 0)
    def _():
        out_acc[...] += out

    @pl.when(step == steps - 1)
    def _():
        rows = out_acc.shape[0] // blocks
        for m in range(blocks):
            out_refs[m % 2 * parts + m // 2][...] = out_acc[m * rows : (m + 1) * rows].astype(BF16)


def run_outputs(place, hidden, w_own, others):
    parts, chunks = len(hidden), len(others)
    count, half, units = w_own.shape
    pair, tokens, width = count // chunks, parts * hidden[0].shape[0], 2 * half
    outs = (shape((tokens // parts // 2, width), BF16),) * (2 * parts)
    column = pl.BlockSpec((tokens // parts, pair * units), lambda i: (0, i))
    return pl.pallas_call(
        functools.partial(outputs_kernel, 2 * parts, parts, chunks),
        grid=(chunks,),
        out_shape=outs,
        in_specs=[
            pl.BlockSpec(memory_space=pltpu.SMEM),
            pl.BlockSpec((pair, half, units), lambda i: (i, 0, 0)),
        ]
        + [column] * parts
        + [held(o) for o in others],
        out_specs=tuple(held(o) for o in outs),
        scratch_shapes=[pltpu.VMEM((tokens, width), F32)],
        compiler_params=pltpu.CompilerParams(vmem_limit_bytes=VMEM_BYTES),
        cost_estimate=cost("outputs"),
        name="outputs",
    )(place, w_own, *hidden, *others)


def rms_back(rows, gain, grad):
    scale = lax.rsqrt(jnp.mean(rows * rows, axis=-1, keepdims=True) + NORM_EPS)
    d_gain = jnp.sum(grad * rows * scale, axis=0, keepdims=True)
    pulled = grad * gain
    mean = jnp.mean(pulled * rows, axis=-1, keepdims=True)
    return scale * pulled - rows * (scale * scale * scale) * mean, d_gain


def body(
    hidden_in,
    positions,
    routes,
    out_grad,
    attn_gain,
    query_weight,
    key_matrix,
    value_matrix,
    out_weight,
    moe_gain,
    router_weight,
    gate_weight,
    up_weight,
    down_weight,
):
    shards, contexts, tensors = (lax.axis_size(a) for a in ("shards", "context", "tensor"))
    shard, context, tensor = (lax.axis_index(a) for a in ("shards", "context", "tensor"))
    owners = shards * contexts
    steps = stepped()
    owner = shard * contexts + context if steps else 0 * shard
    flip = context if steps else 0 * context
    rows, width = hidden_in.shape[1:]
    chunk, quarter = width // owners, rows // tensors
    wide, narrow = query_weight.shape[1], key_matrix.shape[1]
    heads, group = wide // HEAD_SIZE, wide // narrow
    expert_count, local_experts = router_weight.shape[1], gate_weight.shape[0]
    columns = 2 * wide + 2 * narrow
    gates_at = tensor if steps else context * tensors + tensor
    place = jnp.stack([shard, context * local_experts, flip, owner, tensor, gates_at])
    place = place.astype(jnp.int32)

    packed = jnp.concatenate(
        [
            jnp.concatenate([query_weight, key_matrix, value_matrix, out_weight], axis=1),
            jnp.pad(
                jnp.concatenate([attn_gain, moe_gain])[None], ((0, 7), (0, columns - 2 * chunk))
            ),
            jnp.pad(
                router_weight.reshape(8, chunk * expert_count // 8),
                ((0, 0), (0, columns - chunk * expert_count // 8)),
            ),
        ],
        axis=0,
    )
    grad_rows = out_grad[0]
    names = jnp.arange(LANES, dtype=jnp.int32)
    mask = jnp.any(routes[0][:, :, None] == names[None, None, :], axis=1).astype(BF16)
    gathered = gather_owners(packed)
    if steps:
        even, odd = gathered[:4], gathered[4:]
        pieces = [p for pair in zip(even, odd) for p in pair]
        gain_a = jnp.concatenate([p[chunk : chunk + 1, :chunk] for p in pieces], axis=1).astype(F32)
    else:
        stack = gathered[0]
        pieces = [stack[:, :chunk].reshape(width, columns)]
        gain_a = stack[:, chunk, :chunk].reshape(1, width).astype(F32)

    chunks = 2 if local_experts % 2 == 0 else 1
    size = local_experts // chunks
    weights = [lax.all_gather(w, "shards", axis=1, tiled=True) for w in (gate_weight, up_weight)]
    weights.append(down_weight)
    down_other = [swap(down_weight[i * size : (i + 1) * size], "shards", 1) for i in range(chunks)]
    others = [[], [], down_other]

    place_all = positions[0].reshape(contexts, rows)
    own_places = cut(place_all, context, 1).reshape(rows, 1)
    if steps:
        place_all = jnp.concatenate(xor_blocks([place_all[i] for i in range(contexts)], context))
    all_places = place_all.reshape(1, contexts * rows)
    half = HEAD_SIZE // 2
    frequency = ROPE_BASE ** (-2.0 * jnp.arange(half, dtype=F32) / HEAD_SIZE)
    angles = own_places.astype(F32) * frequency[None, :]
    cosine, sine = jnp.cos(angles), jnp.sin(angles)
    cosine = jnp.concatenate([cosine] * 4, axis=1)
    sine = jnp.concatenate([-sine, sine] * 2, axis=1)

    hidden = hidden_in[0]
    hidden_rel = hidden
    if steps:
        hidden_rel = jnp.concatenate(xor_blocks(columns_of(hidden, owners), owner), axis=1)
    normed_a, query, kv, w_qkv = project(
        hidden_rel, gain_a, pieces, cosine, sine, wide, narrow, chunk if steps else width
    )
    kv_all = gather_context(kv)
    attended, lse = attend(query, kv_all, own_places, all_places, heads, group)

    if steps:
        evens = jnp.concatenate([p[:chunk, columns - wide :] for p in even], axis=0)
        bit = 1
        while bit < tensors:
            evens = jnp.concatenate([evens, after(swap(evens, "tensor", bit), query)], axis=0)
            bit *= 2
        w_out = call(
            functools.partial(assemble_kernel, (0, 2, 4, 6, 1, 3, 5, 7), chunk),
            [shape((width, wide * tensors), BF16)],
            (evens, swap(after(evens, attended), "context", 1)),
            "assemble",
            smem=(place,),
        )[0]
        late = [after(p, query) for p in pieces]
        gain_m = [p[chunk : chunk + 1, chunk : 2 * chunk] for p in late]
        gain_m = jnp.concatenate(xor_blocks(gain_m, owner), axis=1).astype(F32)
        router = [p[chunk + 8 : chunk + 16, : chunk * expert_count // 8] for p in late]
        router = jnp.concatenate(xor_blocks(router, owner), axis=0).reshape(width, expert_count)
    else:
        own = pieces[0][:, columns - wide :]
        w_out = jnp.concatenate([own] + [turn(own, k) for k in range(1, tensors)], axis=1)
        gain_m = stack[:, chunk, chunk : 2 * chunk].reshape(1, width).astype(F32)
        router = stack[:, chunk + 8 :, : chunk * expert_count // 8].reshape(width, expert_count)
    router = jnp.pad(router, ((0, 0), (0, LANES - expert_count)))
    attended_all = [attended] + [turn(attended, k) for k in range(1, tensors)]
    middle, normed_m = call(
        middle_kernel,
        (shape(hidden.shape, F32), shape(hidden.shape, BF16)),
        (after(hidden, router, down_other[0]), gain_m, w_out, *attended_all),
        "middle",
    )

    if steps:
        across = swap(normed_m, "context", 2)
        x_blocks = [normed_m, swap(normed_m, "context", 1)]
    else:
        x_blocks = gather_context(normed_m)
    g_blocks = gather_context(jnp.concatenate([grad_rows, mask], axis=1))
    run = lambda xs, gs: run_experts(2, chunks, xs, gs, router, place, weights, others)
    if steps:
        found = [run(x_blocks, g_blocks[:2])]
        across = after(across, found[0][0])
        x_blocks += [across, swap(across, "context", 1)]
        found.append(run(x_blocks[2:], g_blocks[2:]))
    else:
        parts = [
            ([cut(x_blocks[0], i, PART_ROWS)], [cut(g_blocks[0], i, PART_ROWS)])
            for i in range(contexts * rows // PART_ROWS)
        ]
        found = [run(xs, gs) for xs, gs in parts]
    gates = found[0][2] if steps else jnp.concatenate([f[2] for f in found], axis=0)

    def to_quarters(kept, sent, form):
        if steps:
            core = [swap(b, "context", 1) for b in sent]
            send = fold((kept[1], core[1]), place, width, 0)[0]
            return send, fold((kept[0], core[0], swap(send, "context", 2)), place, width, form)
        whole = jnp.concatenate([b for pair in zip(kept, sent) for b in pair], axis=0)
        own = lax.psum_scatter(whole, "context", scatter_dimension=0, tiled=True)
        return own, fold((own,), place, width, form)

    early, d_normed = to_quarters([f[0] for f in found], [f[1] for f in found], tensors)
    hidden_parts = [[f[3] for f in found]] if steps else [[f[3]] for f in found]
    hidden_parts = [[after(h[0], d_normed[0])] + h[1:] for h in hidden_parts]
    outputs = [run_outputs(place, h, down_weight, down_other) for h in hidden_parts]
    if steps:
        outputs = [(outputs[0][i], outputs[0][2 + i]) for i in range(2)]
    dims = gate_weight.shape
    if steps:
        columns_in = [[f[i] for f in found] for i in (3, 4, 5)]
        columns_in[0][0] = after(columns_in[0][0], early)
        grads = run_grads(x_blocks, g_blocks, place, *columns_in, dims, chunks)
    else:
        grads = [
            run_grads(xs, gs, place, [f[3]], [f[4]], [f[5]], dims, chunks)
            for f, (xs, gs) in zip(found, parts)
        ]
        grads = [sum(g.astype(F32) for g in one).astype(BF16) for one in zip(*grads)]

    parts = [d_normed[0]] + [turn(d_normed[k], k) for k in range(1, tensors)]
    outs = (
        shape((quarter, width), F32),
        shape((quarter, width), BF16),
        shape((1, width), F32),
        shape((width, LANES), F32),
        shape((quarter, wide), BF16),
    ) + (shape((quarter, wide + width), BF16),) * (tensors - 1)
    own = lambda lanes: pl.BlockSpec((quarter, lanes), lambda i, at: (at[4], 0))
    gates_own = pl.BlockSpec((quarter, LANES), lambda i, at: (at[5], 0))
    full = lambda a: pl.BlockSpec(a.shape, lambda i, at: (0, 0))
    d_middle, d_attn, d_gain_m, d_router, *d_attended = pl.pallas_call(
        functools.partial(middle_back_kernel, width),
        out_shape=outs,
        grid_spec=pltpu.PrefetchScalarGridSpec(
            num_scalar_prefetch=1,
            grid=(1,),
            in_specs=[own(width), own(width), full(gain_m), own(width), gates_own, full(router), full(w_out)]
            + [full(p) for p in parts],
            out_specs=tuple(full(o) for o in outs),
        ),
        compiler_params=pltpu.CompilerParams(vmem_limit_bytes=VMEM_BYTES),
        cost_estimate=cost("middle_back"),
        name="middle_back",
    )(place, middle, normed_m, gain_m, grad_rows, after(gates, outputs[0][0], grads[0]), router, w_out, *parts)

    came = [swap(grads[i], "shards", 1) for i in (5, 1, 3)]

    d_attended = [turn(d, k) if k else d for k, d in enumerate(d_attended)]
    out_early, moe_out = to_quarters(
        *([after(o[i], d_middle) for o in outputs] for i in range(2)), 0
    )
    d_query, d_kv, d_kv_send = attend_back(
        contexts if steps else 2,
        after(query, came[0], out_early),
        kv_all,
        own_places,
        all_places,
        lse,
        d_attended,
        place,
        cosine,
        sine,
        heads,
        group,
    )
    exchange = lambda x: lax.all_to_all(x, "tensor", 0, 0, tiled=True)
    moe_rows = exchange(moe_out[0].reshape(tensors, quarter, width))
    moe_rows = jnp.sum(moe_rows.astype(F32), axis=0)
    block_out = (cut(middle, tensor, quarter) + RESID_MULT * moe_rows).astype(BF16)
    if steps:
        d_kv = d_kv.astype(F32) + swap(d_kv_send, "context", 1).astype(F32)
        d_kv, d_kv_send = d_kv[:rows], swap(d_kv[rows:].astype(BF16), "context", 2)
    else:
        d_kv = jnp.concatenate([d_kv, d_kv_send], axis=0)
        d_kv = lax.psum_scatter(d_kv, "context", scatter_dimension=0, tiled=True)
        d_kv_send = jnp.zeros_like(d_kv)
    *d_normed, d_lin, d_gain_a = call(
        functools.partial(project_back_kernel, narrow),
        [shape((quarter, width), F32)]
        + [shape((quarter, width), BF16)] * (tensors - 1)
        + [shape((rows, wide + 2 * narrow), BF16), shape((1, width), F32)],
        (after(d_query, came[1], moe_out[0]), d_kv, d_kv_send, cosine[:, :narrow], sine[:, :narrow], w_qkv, hidden_rel),
        "project_back",
        smem=(place,),
        scratch_shapes=[pltpu.VMEM((rows, width), F32)],
    )
    parts = [turn(d_normed[k], k) for k in range(1, tensors)]
    if steps:
        kept, sent = call(
            functools.partial(weights_back_kernel, OWNER_ORDER, chunk),
            [shape((width // 2, columns), BF16)] * 2,
            (normed_a, after(d_lin, moe_rows), attended, d_attn, *d_attended[1:]),
            "weights_back",
            smem=(place,),
            scratch_shapes=[pltpu.VMEM((rows, width), BF16), pltpu.VMEM((width, wide), F32)],
        )
        tie, d_weights = scatter_owners(kept, sent, BF16)
    d_normed = d_normed[0] + sum(p.astype(F32) for p in parts)
    d_rows, _unused = rms_back(
        cut(hidden_rel, tensor, quarter).astype(F32), gain_a, d_normed
    )
    if steps:
        d_rows = jnp.concatenate(xor_blocks(columns_of(d_rows, owners), owner), axis=1)
    in_grad = gather_tensor((d_middle + d_rows).astype(BF16)).astype(F32)

    block_out = exchange(jnp.broadcast_to(after(block_out, d_rows)[None], (tensors, quarter, width)))
    block_out = block_out.reshape(rows, width)

    expert_grads = [
        after(own, d_rows).astype(F32) + other.astype(F32)
        for own, other in ((grads[0], came[1]), (grads[2], came[2]), (grads[4], came[0]))
    ]
    small = jnp.concatenate([d_gain_m, d_router[:, :expert_count].T], axis=0)
    d_gain_a = after(d_gain_a, d_normed)
    if steps:
        small = xor_blocks(columns_of(small, owners), owner)
        small = [
            jnp.concatenate([a, b], axis=0) for a, b in zip(columns_of(d_gain_a, owners), small)
        ]
        small = [jnp.pad(b, ((0, -b.shape[0] % 8), (0, 0))) for b in small]
        kept, sent = (
            jnp.concatenate([small[r] for r in OWNER_ORDER[i : i + 4]], axis=0) for i in (0, 4)
        )
        small = scatter_owners(kept, sent, F32)[1]
    else:
        over = ("shards", "context")
        attn_rows = [d_attn] + [d[:, wide:] for d in d_attended[1:]]
        attn_rows = jnp.concatenate(xor_blocks(attn_rows, tensor), axis=0)
        d_weights = jnp.concatenate([tn(normed_a, d_lin), tn(attn_rows, attended)], axis=1)
        d_weights = lax.psum_scatter(
            d_weights.astype(BF16), over, scatter_dimension=0, tiled=True
        ).astype(F32)
        small = jnp.concatenate([d_gain_a, small], axis=0)
        small = jnp.swapaxes(small.reshape(-1, owners, chunk), 0, 1)
        small = lax.psum_scatter(small, over, scatter_dimension=0)
    small = butterfly(small)
    return (
        block_out[None],
        in_grad[None],
        small[0],
        d_weights[:, :wide],
        d_weights[:, wide : wide + narrow],
        d_weights[:, wide + narrow : wide + 2 * narrow],
        d_weights[:, wide + 2 * narrow :],
        small[1],
        small[2 : 2 + expert_count].T,
        expert_grads[0],
        expert_grads[1],
        expert_grads[2],
    )


def solution(mesh):
    owned = ("shards", "context")
    rows = P("shards", "context", None)
    split = P(owned, "tensor")
    expert = P("context", "shards", "tensor")
    return jax.shard_map(
        body,
        mesh=mesh,
        in_specs=(
            rows,
            P("shards", None),
            rows,
            rows,
            P(owned),
            split,
            split,
            split,
            split,
            P(owned),
            P(owned, None),
            expert,
            expert,
            expert,
        ),
        out_specs=(
            rows,
            rows,
            P(owned),
            split,
            split,
            split,
            split,
            P(owned),
            P(owned, None),
            expert,
            expert,
            expert,
        ),
        check_vma=False,
    )
```

profile of v0, /device:TPU:0, one launch (start us, length us, event | category | flops | bytes accessed | tf_op | source)
XLA Modules:
  0.0 291.6 jit_solution(9866850759764958202)
XLA Ops:
  11.2 3.0 %collective-permute-start = (bf16[144,768]{1,0:T(8,128)(2,1)}, bf16[144,768]{1,0:T(8,128)(2,1)S(1)}, u32[]{:S(2)}, u32[]{:S(2)}) collective-permute-start(bf16[144,768]{1,0:T(8,128)(2,1)} %fusion.9.refs_0_), channel_id=1, source_target_pairs={{0,8},{4,12},{8,0},{12,4},{16,24},{20,28},{24,16},{28,20},{1,9},{5... | collective-permute-start | bytes 663560 | tf_op jit(solution)/shard_map/ppermute | solution.py:69
  26.6 4.3 %collective-permute-done.2.refs_6_ = bf16[144,768]{1,0:T(8,128)(2,1)} collective-permute-done((bf16[144,768]{1,0:T(8,128)(2,1)}, bf16[144,768]{1,0:T(8,128)(2,1)}, u32[]{:S(2)}, u32[]{:S(2)}) %collective-permute-start.2) | collective-permute-done | bytes 221216 | tf_op jit(solution)/shard_map/ppermute | solution.py:69
  40.2 3.4 %project.1 = (bf16[256,1024]{1,0:T(8,128)(2,1)}, bf16[256,256]{1,0:T(8,128)(2,1)}, bf16[256,256]{1,0:T(8,128)(2,1)}, bf16[1024,512]{1,0:T(8,128)(2,1)}) custom-call(bf16[256,1024]{1,0:T(8,128)(2,1)} %copy-done.11, f32[1,1024]{1,0:T(1,128)} %convert_element_type.98.gain_ref, f32[256,128]{1,0:T(8,128)} %pad_maximum_fusion.3.cos_ref, ...), custom_call_target="tpu_custom_call" | custom-call | flops 3449999872 | tf_op jit(solution)/shard_map/project/pallas_call | solution.py:157
  54.8 4.3 %attend.1 = (bf16[256,256]{1,0:T(8,128)(2,1)}, f32[256,4]{1,0:T(8,128)}) custom-call(bf16[256,256]{1,0:T(8,128)(2,1)} %get-tuple-element.139.q_ref, s32[256,1]{1,0:T(8,128)} %copy.64.own_ref, s32[1,1024]{1,0:T(1,128)} %bitcast.58, bf16[256,256]{1,0:T(8,128)(2,1)} %get-tuple-element.104.refs_0_.refs_4_, bf16[256,256]{1,0:T(8,128)(2,1)} %copy-done.46, ...), custom_call_target="tpu_custom_call" | custom-call | flops 4600000000 | tf_op jit(solution)/shard_map/attend/pallas_call | solution.py:157
  59.0 14.2 %collective-permute-done.7 = bf16[1024,256]{1,0:T(8,128)(2,1)S(1)} collective-permute-done((bf16[1024,256]{1,0:T(8,128)(2,1)S(1)}, bf16[1024,256]{1,0:T(8,128)(2,1)S(1)}, u32[]{:S(2)}, u32[]{:S(2)}) %collective-permute-start.7) | collective-permute-done | bytes 524320 | tf_op jit(solution)/shard_map/ppermute | solution.py:38
  75.2 3.2 %collective-permute-start.13 = (bf16[256,256]{1,0:T(8,128)(2,1)}, bf16[256,256]{1,0:T(8,128)(2,1)S(1)}, u32[]{:S(2)}, u32[]{:S(2)}) collective-permute-start(bf16[256,256]{1,0:T(8,128)(2,1)} %get-tuple-element.105.refs_0_.att_ref), channel_id=1, source_target_pairs={{0,2},{1,3},{2,0},{3,1},{4,6},{5,7},{6,4},{7,5},{8,10},{9,11},{10,... | collective-permute-start | bytes 393224 | tf_op jit(solution)/shard_map/ppermute | solution.py:38
  79.6 3.2 %assemble.1.w_ref = bf16[1024,1024]{1,0:T(8,128)(2,1)} custom-call(s32[6]{0:T(128)} %stack.24.place_ref._place_ref, bf16[2048,256]{1,0:T(8,128)(2,1)} %copy-done.25, bf16[2048,256]{1,0:T(8,128)(2,1)} %collective-permute-done.11.odd_ref), custom_call_target="tpu_custom_call" | custom-call | flops 3449999872 | tf_op jit(solution)/shard_map/assemble/pallas_call | solution.py:157
  89.8 3.8 %middle.1 = (f32[256,1024]{1,0:T(8,128)}, bf16[256,1024]{1,0:T(8,128)(2,1)}) custom-call(bf16[256,1024]{1,0:T(8,128)(2,1)} %bitcast.50, f32[1,1024]{1,0:T(1,128)} %convert_element_type.101.gain_ref, bf16[1024,1024]{1,0:T(8,128)(2,1)} %assemble.1.w_ref, bf16[256,256]{1,0:T(8,128)(2,1)} %get-tuple-element.105.refs_0_.att_ref, bf16[256,256]{1,0:T(8,128)(2,1)} %copy-done.49, ...), custom_call_target="tpu_custom_call" | custom-call | flops 4600000000 | tf_op jit(solution)/shard_map/middle/pallas_call | solution.py:157
  94.7 5.5 %collective-permute-done.17.refs_8_.refs_3_ = bf16[4,512,128]{2,1,0:T(8,128)(2,1)S(1)} collective-permute-done((bf16[4,512,128]{2,1,0:T(8,128)(2,1)S(1)}, bf16[4,512,128]{2,1,0:T(8,128)(2,1)S(1)}, u32[]{:S(2)}, u32[]{:S(2)}) %collective-permute-start.17) | collective-permute-done | bytes 524320 | tf_op jit(solution)/shard_map/ppermute | solution.py:38
  101.8 12.8 %experts.2 = (bf16[256,1152]{1,0:T(8,128)(2,1)}, bf16[256,1152]{1,0:T(8,128)(2,1)}, f32[512,128]{1,0:T(8,128)}, bf16[512,1024]{1,0:T(8,128)(2,1)}, bf16[512,1024]{1,0:T(8,128)(2,1)}, /*index=5*/bf16[512,1024]{1,0:T(8,128)(2,1)}) custom-call(s32[6]{0:T(128)} %stack.24.place_ref._place_ref, bf16[1024,128]{1,0:T(8,128)(2,1)} %pad.39.router_ref, ...), custom_call_target="tpu_custom_call" | custom-call | flops 13799999488 | tf_op jit(solution)/shard_map/experts/pallas_call | solution.py:532
  117.6 12.6 %experts.3 = (bf16[256,1152]{1,0:T(8,128)(2,1)}, bf16[256,1152]{1,0:T(8,128)(2,1)}, f32[512,128]{1,0:T(8,128)}, bf16[512,1024]{1,0:T(8,128)(2,1)}, bf16[512,1024]{1,0:T(8,128)(2,1)}, /*index=5*/bf16[512,1024]{1,0:T(8,128)(2,1)}) custom-call(s32[6]{0:T(128)} %stack.24.place_ref._place_ref, bf16[1024,128]{1,0:T(8,128)(2,1)} %pad.39.router_ref, ...), custom_call_target="tpu_custom_call" | custom-call | flops 13799999488 | tf_op jit(solution)/shard_map/experts/pallas_call | solution.py:532
  135.9 12.0 %grads.1 = (bf16[8,512,128]{2,1,0:T(8,128)(2,1)}, bf16[8,512,128]{2,1,0:T(8,128)(2,1)}, bf16[8,512,128]{2,1,0:T(8,128)(2,1)}, bf16[8,512,128]{2,1,0:T(8,128)(2,1...) custom-call(s32[6]{0:T(128)} %stack.24.place_ref._place_ref, ...), custom_call_target="tpu_custom_call" | custom-call | flops 13799999488 | tf_op jit(solution)/shard_map/grads/pallas_call | solution.py:581
  159.1 6.6 %outputs.1 = (bf16[256,1024]{1,0:T(8,128)(2,1)}, bf16[256,1024]{1,0:T(8,128)(2,1)}, bf16[256,1024]{1,0:T(8,128)(2,1)}, bf16[256,1024]{1,0:T(8,128)(2,1)}) custom-call(s32[6]{0:T(128)} %stack.24.place_ref._place_ref, bf16[8,512,128]{2,1,0:T(8,128)(2,1)} %wd0_ref.1, bf16[512,1024]{1,0:T(8,128)(2,1)} %get-tuple-element.120.refs_0_.refs_8_, ...), custom_call_target="tpu_custom_call" | custom-call | flops 10350000128 | tf_op jit(solution)/shard_map/outputs/pallas_call | solution.py:622
  165.7 3.2 %collective-permute-done.26.refs_2_ = bf16[64,1152]{1,0:T(8,128)(2,1)S(1)} collective-permute-done((bf16[64,1152]{1,0:T(8,128)(2,1)}, bf16[64,1152]{1,0:T(8,128)(2,1)S(1)}, u32[]{:S(2)}, u32[]{:S(2)}) %collective-permute-start.26) | collective-permute-done | bytes 147488 | tf_op jit(solution)/shard_map/ppermute | solution.py:38
  169.7 4.5 %middle_back.1 = (f32[64,1024]{1,0:T(8,128)}, bf16[64,1024]{1,0:T(8,128)(2,1)}, f32[1,1024]{1,0:T(1,128)}, f32[1024,128]{1,0:T(8,128)}, bf16[64,256]{1,0:T(8,128...) custom-call(s32[6]{0:T(128)} %stack.24.place_ref._place_ref, ...), custom_call_target="tpu_custom_call" | custom-call | flops 5175000064 | tf_op jit(solution)/shard_map/middle_back/pallas_call | solution.py:825
  186.8 7.9 %collective-permute-done.33.refs_2_ = bf16[64,1280]{1,0:T(8,128)(2,1)S(1)} collective-permute-done((bf16[64,1280]{1,0:T(8,128)(2,1)}, bf16[64,1280]{1,0:T(8,128)(2,1)S(1)}, u32[]{:S(2)}, u32[]{:S(2)}) %collective-permute-start.33) | collective-permute-done | bytes 163872 | tf_op jit(solution)/shard_map/ppermute | solution.py:38
  195.8 6.4 %attend_back.1 = (bf16[256,256]{1,0:T(8,128)(2,1)}, bf16[512,256]{1,0:T(8,128)(2,1)}, bf16[512,256]{1,0:T(8,128)(2,1)}) custom-call(s32[6]{0:T(128)} %stack.24.place_ref._place_ref, bf16[256,256]{1,0:T(8,128)(2,1)} %get-tuple-element.139.q_ref, s32[256,1]{1,0:T(8,128)} %copy.64.own_ref, s32[1,1024]{1,0:T(1,128)} %bitcast.59, ...), custom_call_target="tpu_custom_call" | custom-call | flops 6899999744 | tf_op jit(solution)/shard_map/attend_back/pallas_call | solution.py:157
  212.0 3.1 %project_back.1 = (f32[64,1024]{1,0:T(8,128)}, bf16[64,1024]{1,0:T(8,128)(2,1)}, bf16[64,1024]{1,0:T(8,128)(2,1)}, bf16[64,1024]{1,0:T(8,128)(2,1)}, bf16[256,512]{1,0:T(8,128)(2,1)}, /*index=5*/f32[1,1024]{1,0:T(1,128)}) custom-call(s32[6]{0:T(128)} %stack.24.place_ref._place_ref, bf16[256,256]{1,0:T(8,128)(2,1)} %get-tuple-element.147.dq_ref, ...), custom_call_target="tpu_custom_call" | custom-call | flops 3449999872 | tf_op jit(solution)/shard_map/project_back/pallas_call | solution.py:157
  220.7 3.7 %all-to-all-start = ((bf16[4,64,1024]{2,1,0:T(8,128)(2,1)}), bf16[4,64,1024]{2,1,0:T(8,128)(2,1)S(1)}, u32[]{:S(2)}, u32[]{:S(2)}) async-start(bf16[4,64,1024]{2,1,0:T(8,128)(2,1)} %bitcast.15), calls=%async_computation | async-start | bytes 1048576 | tf_op jit(solution)/shard_map/all_to_all | solution.py:860
  224.5 9.4 %collective-permute-done.39 = bf16[64,1024]{1,0:T(8,128)(2,1)S(1)} collective-permute-done((bf16[64,1024]{1,0:T(8,128)(2,1)}, bf16[64,1024]{1,0:T(8,128)(2,1)S(1)}, u32[]{:S(2)}, u32[]{:S(2)}) %collective-permute-start.39) | collective-permute-done | bytes 131104 | tf_op jit(solution)/shard_map/ppermute | solution.py:38
  236.2 5.6 %collective-permute-start.41 = (bf16[64,1024]{1,0:T(8,128)(2,1)}, bf16[64,1024]{1,0:T(8,128)(2,1)S(1)}, u32[]{:S(2)}, u32[]{:S(2)}) collective-permute-start(bf16[64,1024]{1,0:T(8,128)(2,1)} %get-tuple-element.210), channel_id=1, source_target_pairs={{0,1},{1,0},{2,3},{3,2},{4,5},{5,4},{6,7},{7,6},{8,9},{9,8},{10,11... | collective-permute-start | bytes 393224 | tf_op jit(solution)/shard_map/ppermute | solution.py:38
  252.2 3.2 %weights_back.1 = (bf16[512,768]{1,0:T(8,128)(2,1)}, bf16[512,768]{1,0:T(8,128)(2,1)}) custom-call(s32[6]{0:T(128)} %stack.24.place_ref._place_ref, bf16[256,1024]{1,0:T(8,128)(2,1)} %get-tuple-element.160.norm_ref, bf16[256,512]{1,0:T(8,128)(2,1)} %get-tuple-element.162.dlin_ref, bf16[256,256]{1,0:T(8,128)(2,1)} %get-tuple-element.105.refs_0_.att_ref, ...), custom_call_target="tpu_custom_call" | custom-call | flops 3449999872 | tf_op jit(solution)/shard_map/weights_back/pallas_call | solution.py:157
  262.9 3.5 %all-to-all-start.1 = ((bf16[4,64,1024]{2,1,0:T(8,128)(2,1)}), bf16[4,64,1024]{2,1,0:T(8,128)(2,1)S(1)}, u32[]{:S(2)}, u32[]{:S(2)}) async-start(bf16[4,64,1024]{2,1,0:T(8,128)(2,1)} %broadcast_in_dim.29), calls=%async_computation.1 | async-start | bytes 1048576 | tf_op jit(solution)/shard_map/all_to_all | solution.py:860
  269.2 7.5 %collective-permute-done.50 = bf16[256,768]{1,0:T(8,128)(2,1)S(1)} collective-permute-done((bf16[256,768]{1,0:T(8,128)(2,1)S(1)}, bf16[256,768]{1,0:T(8,128)(2,1)S(1)}, u32[]{:S(2)}, u32[]{:S(2)}) %collective-permute-start.50) | collective-permute-done | bytes 393248 | tf_op jit(solution)/shard_map/ppermute | solution.py:38
  (347 shorter events, 129.9 us)
Async XLA Ops:
  7.2 93.0 %all-gather.3.cloned.1.call-start = ((), (), s32[]{:S(2)}) async-start(), calls=%async_computation.2 | async-start | bytes 3145728 | tf_op jit(solution)/shard_map/all_gather | solution.py:708
  7.9 92.3 %all-gather.5.cloned.1.call-start = ((), (), s32[]{:S(2)}) async-start(), calls=%async_computation.3 | async-start | bytes 3145728 | tf_op jit(solution)/shard_map/all_gather | solution.py:708
  15.7 15.2 %collective-permute-start.2 = (bf16[144,768]{1,0:T(8,128)(2,1)}, bf16[144,768]{1,0:T(8,128)(2,1)}, u32[]{:S(2)}, u32[]{:S(2)}) collective-permute-start(bf16[144,768]{1,0:T(8,128)(2,1)} %fusion.9.refs_0_), channel_id=1, source_target_pairs={{0,24},{4,28},{8,16},{12,20},{16,8},{20,12},{24,0},{28,4},{1,25},{... | collective-permute-start | bytes 663560 | tf_op jit(solution)/shard_map/ppermute | solution.py:69
  15.7 21.6 %collective-permute-start.4 = (bf16[144,768]{1,0:T(8,128)(2,1)}, bf16[144,768]{1,0:T(8,128)(2,1)S(1)}, u32[]{:S(2)}, u32[]{:S(2)}) collective-permute-start(bf16[144,768]{1,0:T(8,128)(2,1)} %fusion.9.refs_0_), channel_id=1, source_target_pairs={{0,4},{4,0},{8,12},{12,8},{1,5},{5,1},{9,13},{13,9},{2,6},{6,2},{1... | collective-permute-start | bytes 663560 | tf_op jit(solution)/shard_map/ppermute | solution.py:38
  17.1 83.1 %collective-permute-start.16 = (bf16[256,1152]{1,0:T(8,128)(2,1)S(1)}, bf16[256,1152]{1,0:T(8,128)(2,1)}, u32[]{:S(2)}, u32[]{:S(2)}) collective-permute-start(bf16[256,1152]{1,0:T(8,128)(2,1)S(1)} %pad_maximum_fusion.1.refs_2_.refs_4_), channel_id=1, source_target_pairs={{0,4},{4,0},{8,12},{12,8},{1,5},{5,1},{9,13},{13,9},{2,6},{6,2},{1... | collective-permute-start | bytes 1769480 | tf_op jit(solution)/shard_map/ppermute | solution.py:38
  24.5 69.1 %collective-permute-start.21 = (bf16[256,1152]{1,0:T(8,128)(2,1)S(1)}, bf16[256,1152]{1,0:T(8,128)(2,1)}, u32[]{:S(2)}, u32[]{:S(2)}) collective-permute-start(bf16[256,1152]{1,0:T(8,128)(2,1)S(1)} %pad_maximum_fusion.1.refs_2_.refs_4_), channel_id=1, source_target_pairs={{0,8},{4,12},{8,0},{12,4},{1,9},{5,13},{9,1},{13,5},{2,10},{6,14},... | collective-permute-start | bytes 1769480 | tf_op jit(solution)/shard_map/ppermute | solution.py:38
  46.8 26.5 %collective-permute-start.7 = (bf16[1024,256]{1,0:T(8,128)(2,1)S(1)}, bf16[1024,256]{1,0:T(8,128)(2,1)S(1)}, u32[]{:S(2)}, u32[]{:S(2)}) collective-permute-start(bf16[1024,256]{1,0:T(8,128)(2,1)S(1)} %get-tuple-element.265), channel_id=1, source_target_pairs={{0,2},{1,3},{2,0},{3,1},{4,6},{5,7},{6,4},{7,5},{8,10},{9,11},{10,... | collective-permute-start | bytes 1572872 | tf_op jit(solution)/shard_map/ppermute | solution.py:38
  51.6 23.6 %collective-permute-start.5 = (bf16[4,512,128]{2,1,0:T(8,128)(2,1)S(1)}, bf16[4,512,128]{2,1,0:T(8,128)(2,1)}, u32[]{:S(2)}, u32[]{:S(2)}) collective-permute-start(bf16[4,512,128]{2,1,0:T(8,128)(2,1)S(1)} %get-tuple-element.253), channel_id=1, source_target_pairs={{0,16},{16,0},{1,17},{17,1},{2,18},{18,2},{3,19},{19,3},{4,20},{20... | collective-permute-start | bytes 1572872 | tf_op jit(solution)/shard_map/ppermute | solution.py:38
  83.5 16.7 %collective-permute-start.17 = (bf16[4,512,128]{2,1,0:T(8,128)(2,1)S(1)}, bf16[4,512,128]{2,1,0:T(8,128)(2,1)S(1)}, u32[]{:S(2)}, u32[]{:S(2)}) collective-permute-start(bf16[4,512,128]{2,1,0:T(8,128)(2,1)S(1)} %get-tuple-element.252), channel_id=1, source_target_pairs={{0,16},{16,0},{1,17},{17,1},{2,18},{18,2},{3,19},{19,3},{4,20},{20... | collective-permute-start | bytes 1572872 | tf_op jit(solution)/shard_map/ppermute | solution.py:38
  93.7 21.0 %collective-permute-start.22 = (bf16[256,1152]{1,0:T(8,128)(2,1)}, bf16[256,1152]{1,0:T(8,128)(2,1)S(1)}, u32[]{:S(2)}, u32[]{:S(2)}) collective-permute-start(bf16[256,1152]{1,0:T(8,128)(2,1)} %collective-permute-done.21.refs_2_.refs_6_), channel_id=1, source_target_pairs={{0,4},{4,0},{8,12},{12,8},{1,5},{5,1},{9,13},{13,9},{2,6},{6,2},{1... | collective-permute-start | bytes 1769480 | tf_op jit(solution)/shard_map/ppermute | solution.py:38
  94.2 20.4 %collective-permute-start.19 = (bf16[256,1024]{1,0:T(8,128)(2,1)}, bf16[256,1024]{1,0:T(8,128)(2,1)}, u32[]{:S(2)}, u32[]{:S(2)}) collective-permute-start(bf16[256,1024]{1,0:T(8,128)(2,1)} %get-tuple-element.108.refs_0_.norm_ref), channel_id=1, source_target_pairs={{0,8},{4,12},{8,0},{12,4},{1,9},{5,13},{9,1},{13,5},{2,10},{6,14},... | collective-permute-start | bytes 1572872 | tf_op jit(solution)/shard_map/ppermute | solution.py:38
  130.3 19.4 %collective-permute-start.18 = (bf16[256,1152]{1,0:T(8,128)(2,1)S(1)}, bf16[256,1152]{1,0:T(8,128)(2,1)S(1)}, u32[]{:S(2)}, u32[]{:S(2)}) collective-permute-start(bf16[256,1152]{1,0:T(8,128)(2,1)S(1)} %copy-done.29), channel_id=1, source_target_pairs={{0,4},{4,0},{8,12},{12,8},{1,5},{5,1},{9,13},{13,9},{2,6},{6,2},{1... | collective-permute-start | bytes 1769480 | tf_op jit(solution)/shard_map/ppermute | solution.py:38
  135.7 15.6 %collective-permute-start.24 = (bf16[256,1152]{1,0:T(8,128)(2,1)}, bf16[256,1152]{1,0:T(8,128)(2,1)S(1)}, u32[]{:S(2)}, u32[]{:S(2)}) collective-permute-start(bf16[256,1152]{1,0:T(8,128)(2,1)} %fold.4), channel_id=1, source_target_pairs={{0,8},{4,12},{8,0},{12,4},{1,9},{5,13},{9,1},{13,5},{2,10},{6,14},... | collective-permute-start | bytes 1769480 | tf_op jit(solution)/shard_map/ppermute | solution.py:38
  147.9 37.5 %collective-permute-start.31 = (bf16[8,512,128]{2,1,0:T(8,128)(2,1)}, bf16[8,512,128]{2,1,0:T(8,128)(2,1)S(1)}, u32[]{:S(2)}, u32[]{:S(2)}) collective-permute-start(bf16[8,512,128]{2,1,0:T(8,128)(2,1)} %get-tuple-element.138), channel_id=1, source_target_pairs={{0,16},{16,0},{1,17},{17,1},{2,18},{18,2},{3,19},{19,3},{4,20},{20... | collective-permute-start | bytes 3145736 | tf_op jit(solution)/shard_map/ppermute | solution.py:38
  175.7 35.6 %collective-permute-start.35 = (bf16[8,512,128]{2,1,0:T(8,128)(2,1)}, bf16[8,512,128]{2,1,0:T(8,128)(2,1)S(1)}, u32[]{:S(2)}, u32[]{:S(2)}) collective-permute-start(bf16[8,512,128]{2,1,0:T(8,128)(2,1)} %get-tuple-element.146), channel_id=1, source_target_pairs={{0,16},{16,0},{1,17},{17,1},{2,18},{18,2},{3,19},{19,3},{4,20},{20... | collective-permute-start | bytes 3145736 | tf_op jit(solution)/shard_map/ppermute | solution.py:38
  179.6 15.2 %collective-permute-start.33 = (bf16[64,1280]{1,0:T(8,128)(2,1)}, bf16[64,1280]{1,0:T(8,128)(2,1)S(1)}, u32[]{:S(2)}, u32[]{:S(2)}) collective-permute-start(bf16[64,1280]{1,0:T(8,128)(2,1)} %get-tuple-element.143), channel_id=1, source_target_pairs={{0,2},{1,3},{2,0},{3,1},{4,6},{5,7},{6,4},{7,5},{8,10},{9,11},{10,... | collective-permute-start | bytes 491528 | tf_op jit(solution)/shard_map/ppermute | solution.py:38
  185.4 62.9 %collective-permute-start.52 = (bf16[8,512,128]{2,1,0:T(8,128)(2,1)}, bf16[8,512,128]{2,1,0:T(8,128)(2,1)}, u32[]{:S(2)}, u32[]{:S(2)}) collective-permute-start(bf16[8,512,128]{2,1,0:T(8,128)(2,1)} %get-tuple-element.169), channel_id=1, source_target_pairs={{0,16},{16,0},{1,17},{17,1},{2,18},{18,2},{3,19},{19,3},{4,20},{20... | collective-permute-start | bytes 3145736 | tf_op jit(solution)/shard_map/ppermute | solution.py:38
  186.8 20.5 %collective-permute-start.28 = (bf16[256,1024]{1,0:T(8,128)(2,1)S(1)}, bf16[256,1024]{1,0:T(8,128)(2,1)S(1)}, u32[]{:S(2)}, u32[]{:S(2)}) collective-permute-start(bf16[256,1024]{1,0:T(8,128)(2,1)S(1)} %copy-done.33), channel_id=1, source_target_pairs={{0,4},{4,0},{8,12},{12,8},{1,5},{5,1},{9,13},{13,9},{2,6},{6,2},{1... | collective-permute-start | bytes 1572872 | tf_op jit(solution)/shard_map/ppermute | solution.py:38
  217.6 16.2 %collective-permute-start.39 = (bf16[64,1024]{1,0:T(8,128)(2,1)}, bf16[64,1024]{1,0:T(8,128)(2,1)S(1)}, u32[]{:S(2)}, u32[]{:S(2)}) collective-permute-start(bf16[64,1024]{1,0:T(8,128)(2,1)} %get-tuple-element.153), channel_id=1, source_target_pairs={{0,2},{1,3},{2,0},{3,1},{4,6},{5,7},{6,4},{7,5},{8,10},{9,11},{10,... | collective-permute-start | bytes 393224 | tf_op jit(solution)/shard_map/ppermute | solution.py:38
  218.4 15.4 %collective-permute-start.40 = (bf16[64,1024]{1,0:T(8,128)(2,1)}, bf16[64,1024]{1,0:T(8,128)(2,1)S(1)}, u32[]{:S(2)}, u32[]{:S(2)}) collective-permute-start(bf16[64,1024]{1,0:T(8,128)(2,1)} %get-tuple-element.154), channel_id=1, source_target_pairs={{0,3},{1,2},{2,1},{3,0},{4,7},{5,6},{6,5},{7,4},{8,11},{9,10},{10,... | collective-permute-start | bytes 393224 | tf_op jit(solution)/shard_map/ppermute | solution.py:38
  220.7 31.4 %all-to-all-start = ((bf16[4,64,1024]{2,1,0:T(8,128)(2,1)}), bf16[4,64,1024]{2,1,0:T(8,128)(2,1)S(1)}, u32[]{:S(2)}, u32[]{:S(2)}) async-start(bf16[4,64,1024]{2,1,0:T(8,128)(2,1)} %bitcast.15), calls=%async_computation | async-start | bytes 1048576 | tf_op jit(solution)/shard_map/all_to_all | solution.py:860
  236.2 19.2 %collective-permute-start.41 = (bf16[64,1024]{1,0:T(8,128)(2,1)}, bf16[64,1024]{1,0:T(8,128)(2,1)S(1)}, u32[]{:S(2)}, u32[]{:S(2)}) collective-permute-start(bf16[64,1024]{1,0:T(8,128)(2,1)} %get-tuple-element.210), channel_id=1, source_target_pairs={{0,1},{1,0},{2,3},{3,2},{4,5},{5,4},{6,7},{7,6},{8,9},{9,8},{10,11... | collective-permute-start | bytes 393224 | tf_op jit(solution)/shard_map/ppermute | solution.py:38
  241.8 25.6 %collective-permute-start.43 = (bf16[64,1024]{1,0:T(8,128)(2,1)}, bf16[64,1024]{1,0:T(8,128)(2,1)S(1)}, u32[]{:S(2)}, u32[]{:S(2)}) collective-permute-start(bf16[64,1024]{1,0:T(8,128)(2,1)} %get-tuple-element.210), channel_id=1, source_target_pairs={{0,3},{1,2},{2,1},{3,0},{4,7},{5,6},{6,5},{7,4},{8,11},{9,10},{10,... | collective-permute-start | bytes 393224 | tf_op jit(solution)/shard_map/ppermute | solution.py:38
  262.9 17.4 %all-to-all-start.1 = ((bf16[4,64,1024]{2,1,0:T(8,128)(2,1)}), bf16[4,64,1024]{2,1,0:T(8,128)(2,1)S(1)}, u32[]{:S(2)}, u32[]{:S(2)}) async-start(bf16[4,64,1024]{2,1,0:T(8,128)(2,1)} %broadcast_in_dim.29), calls=%async_computation.1 | async-start | bytes 1048576 | tf_op jit(solution)/shard_map/all_to_all | solution.py:860
  (85 other events, 553.1 us)
Sparse Core Ops, SparseCore 0:
  9.6 39.1 all-gather.2
  50.3 41.1 all-gather.4
where the time goes:
time: 293 us; the launch traced here: 292 us
  Pallas kernels  85.3 us (29%)
  waiting for transfers between devices  70.2 us (24%)
  starting transfers between devices  66.2 us (23%)
  local copies, waits for them, and re-layouts  29 us (10%)
  other arithmetic  26 us (9%)
  between operations  15 us (5%)
    ppermute x48, waiting for transfers between devices, swap(): return lax.ppermute(x, axis, [(i, i ^ bit) for i in range(devices)])  60.8 us
    ppermute x48, starting transfers between devices, swap(): return lax.ppermute(x, axis, [(i, i ^ bit) for i in range(devices)])  51.6 us
    pallas_call x11, Pallas kernels, call(): pl.pallas_call(kernel, out_shape=tuple(out_shape), in_specs=specs, out_sp...  37 us
    pallas_call x2, Pallas kernels, run_experts(): pl.pallas_call(functools.partial(experts_kernel, blocks, len(x_blocks), [...  25.3 us
    unnamed x120, local copies, waits for them, and re-layouts  17.7 us
    pallas_call x1, Pallas kernels, run_grads(): pl.pallas_call(functools.partial(grads_kernel, len(x_blocks), parts, widt...  12 us
    all_to_all x2, starting transfers between devices, body(): exchange = lambda x: lax.all_to_all(x, 'tensor', 0, 0, tiled=True)  7.2 us
    pallas_call x1, Pallas kernels, run_outputs(): pl.pallas_call(functools.partial(outputs_kernel, 2 * parts, parts, chunks...  6.57 us
  transfers between devices with their start and end apart: 57, of which 19 were waited for; matrix products, arithmetic and copies ran while one was open for 15% of the time, Pallas kernels for 25%

commit v1 on v0

--- a/solution.py
+++ b/solution.py
@@ -883,7 +883,7 @@
         kept, sent = call(
             functools.partial(weights_back_kernel, OWNER_ORDER, chunk),
             [shape((width // 2, columns), BF16)] * 2,
-            (normed_a, after(d_lin, moe_rows), attended, d_attn, *d_attended[1:]),
+            (normed_a, after(d_lin, parts[0]), attended, d_attn, *d_attended[1:]),
             "weights_back",
             smem=(place,),
             scratch_shapes=[pltpu.VMEM((rows, width), BF16), pltpu.VMEM((width, wide), F32)],
@@ -895,17 +895,17 @@
     )
     if steps:
         d_rows = jnp.concatenate(xor_blocks(columns_of(d_rows, owners), owner), axis=1)
-    in_grad = gather_tensor((d_middle + d_rows).astype(BF16)).astype(F32)
-
-    block_out = exchange(jnp.broadcast_to(after(block_out, d_rows)[None], (tensors, quarter, width)))
-    block_out = block_out.reshape(rows, width)
+    both = jnp.concatenate([(d_middle + d_rows).astype(BF16), block_out], axis=1)
+    late = both
+    both = gather_tensor(both)
+    in_grad, block_out = both[:, :width].astype(F32), both[:, width:]
 
     expert_grads = [
-        after(own, d_rows).astype(F32) + other.astype(F32)
+        after(own, late).astype(F32) + other.astype(F32)
         for own, other in ((grads[0], came[1]), (grads[2], came[2]), (grads[4], came[0]))
     ]
     small = jnp.concatenate([d_gain_m, d_router[:, :expert_count].T], axis=0)
-    d_gain_a = after(d_gain_a, d_normed)
+    d_gain_a = after(d_gain_a, late)
     if steps:
         small = xor_blocks(columns_of(small, owners), owner)
         small = [

time: 293 us -> 292 us (level)
  starting transfers between devices: 66.2 us -> 61 us
  waiting for transfers between devices: 70.2 us -> 75.2 us
    ppermute x2, waiting for transfers between devices: 2.64 us -> 9.55 us  [butterfly(): lax.ppermute(x, 'tensor', [(i, i ^ bit) for i in range(lax.axis_size('ten...]
    ppermute x48, waiting for transfers between devices: 60.8 us -> 56.5 us  [swap(): return lax.ppermute(x, axis, [(i, i ^ bit) for i in range(devices)])]
    all_to_all x2 -> x1, starting transfers between devices: 7.2 us -> 3.73 us  [body(): exchange = lambda x: lax.all_to_all(x, 'tensor', 0, 0, tiled=True)]
    unnamed x120 -> x123, local copies, waits for them, and re-layouts: 17.7 us -> 16.8 us
  transfers between devices with their start and end apart: 57 -> 56, of which waited for: 19 -> 21; matrix products, arithmetic and copies ran while one was open for 15% -> 15% of each run, Pallas kernels for 25% -> 25%
where the time goes in v1:
time: 292 us; the launch traced here: 291 us
  Pallas kernels  85.4 us (29%)
  waiting for transfers between devices  75.2 us (26%)
  starting transfers between devices  61 us (21%)
  local copies, waits for them, and re-layouts  27.5 us (9%)
  other arithmetic  26.8 us (9%)
  between operations  15 us (5%)
    ppermute x48, waiting for transfers between devices, swap(): return lax.ppermute(x, axis, [(i, i ^ bit) for i in range(devices)])  56.5 us
    ppermute x48, starting transfers between devices, swap(): return lax.ppermute(x, axis, [(i, i ^ bit) for i in range(devices)])  52 us
    pallas_call x11, Pallas kernels, call(): pl.pallas_call(kernel, out_shape=tuple(out_shape), in_specs=specs, out_sp...  37 us
    pallas_call x2, Pallas kernels, run_experts(): pl.pallas_call(functools.partial(experts_kernel, blocks, len(x_blocks), [...  25.4 us
    unnamed x123, local copies, waits for them, and re-layouts  16.8 us
    pallas_call x1, Pallas kernels, run_grads(): pl.pallas_call(functools.partial(grads_kernel, len(x_blocks), parts, widt...  11.9 us
    ppermute x2, waiting for transfers between devices, butterfly(): lax.ppermute(x, 'tensor', [(i, i ^ bit) for i in range(lax.axis_size('ten...  9.55 us
    add x3, other arithmetic, body(): after(own, late).astype(F32) + other.astype(F32)  7.03 us
  transfers between devices with their start and end apart: 56, of which 21 were waited for; matrix products, arithmetic and copies ran while one was open for 15% of the time, Pallas kernels for 25%

profile of v1, /device:TPU:0, one launch (start us, length us, event | category | flops | bytes accessed | tf_op | source)
XLA Modules:
  0.0 291.0 jit_solution(700490396097096886)
XLA Ops:
  26.6 4.3 %collective-permute-done.2.refs_6_ = bf16[144,768]{1,0:T(8,128)(2,1)} collective-permute-done((bf16[144,768]{1,0:T(8,128)(2,1)}, bf16[144,768]{1,0:T(8,128)(2,1)}, u32[]{:S(2)}, u32[]{:S(2)}) %collective-permute-start.2) | collective-permute-done | bytes 221216 | tf_op jit(solution)/shard_map/ppermute | solution.py:69
  40.2 3.4 %project.1 = (bf16[256,1024]{1,0:T(8,128)(2,1)}, bf16[256,256]{1,0:T(8,128)(2,1)}, bf16[256,256]{1,0:T(8,128)(2,1)}, bf16[1024,512]{1,0:T(8,128)(2,1)}) custom-call(bf16[256,1024]{1,0:T(8,128)(2,1)} %copy-done.12, f32[1,1024]{1,0:T(1,128)} %convert_element_type.98.gain_ref, f32[256,128]{1,0:T(8,128)} %pad_maximum_fusion.4.cos_ref, ...), custom_call_target="tpu_custom_call" | custom-call | flops 3449999872 | tf_op jit(solution)/shard_map/project/pallas_call | solution.py:157
  54.9 4.3 %attend.1 = (bf16[256,256]{1,0:T(8,128)(2,1)}, f32[256,4]{1,0:T(8,128)}) custom-call(bf16[256,256]{1,0:T(8,128)(2,1)} %get-tuple-element.135.q_ref, s32[256,1]{1,0:T(8,128)} %copy.64.own_ref, s32[1,1024]{1,0:T(1,128)} %bitcast.55, bf16[256,256]{1,0:T(8,128)(2,1)} %get-tuple-element.103.refs_0_.refs_4_, bf16[256,256]{1,0:T(8,128)(2,1)} %copy-done.48, ...), custom_call_target="tpu_custom_call" | custom-call | flops 4600000000 | tf_op jit(solution)/shard_map/attend/pallas_call | solution.py:157
  59.1 14.2 %collective-permute-done.7 = bf16[1024,256]{1,0:T(8,128)(2,1)S(1)} collective-permute-done((bf16[1024,256]{1,0:T(8,128)(2,1)S(1)}, bf16[1024,256]{1,0:T(8,128)(2,1)S(1)}, u32[]{:S(2)}, u32[]{:S(2)}) %collective-permute-start.7) | collective-permute-done | bytes 524320 | tf_op jit(solution)/shard_map/ppermute | solution.py:38
  75.2 3.2 %collective-permute-start.13 = (bf16[256,256]{1,0:T(8,128)(2,1)}, bf16[256,256]{1,0:T(8,128)(2,1)S(1)}, u32[]{:S(2)}, u32[]{:S(2)}) collective-permute-start(bf16[256,256]{1,0:T(8,128)(2,1)} %get-tuple-element.104.refs_0_.att_ref), channel_id=1, source_target_pairs={{0,2},{1,3},{2,0},{3,1},{4,6},{5,7},{6,4},{7,5},{8,10},{9,11},{10,... | collective-permute-start | bytes 393224 | tf_op jit(solution)/shard_map/ppermute | solution.py:38
  79.6 3.2 %assemble.1.w_ref = bf16[1024,1024]{1,0:T(8,128)(2,1)} custom-call(s32[6]{0:T(128)} %stack.24.place_ref._place_ref, bf16[2048,256]{1,0:T(8,128)(2,1)} %copy-done.26, bf16[2048,256]{1,0:T(8,128)(2,1)} %collective-permute-done.11.odd_ref), custom_call_target="tpu_custom_call" | custom-call | flops 3449999872 | tf_op jit(solution)/shard_map/assemble/pallas_call | solution.py:157
  89.9 3.8 %middle.1 = (f32[256,1024]{1,0:T(8,128)}, bf16[256,1024]{1,0:T(8,128)(2,1)}) custom-call(bf16[256,1024]{1,0:T(8,128)(2,1)} %bitcast.48, f32[1,1024]{1,0:T(1,128)} %convert_element_type.101.gain_ref, bf16[1024,1024]{1,0:T(8,128)(2,1)} %assemble.1.w_ref, bf16[256,256]{1,0:T(8,128)(2,1)} %get-tuple-element.104.refs_0_.att_ref, bf16[256,256]{1,0:T(8,128)(2,1)} %copy-done.51, ...), custom_call_target="tpu_custom_call" | custom-call | flops 4600000000 | tf_op jit(solution)/shard_map/middle/pallas_call | solution.py:157
  94.7 5.5 %collective-permute-done.17.refs_8_.refs_3_ = bf16[4,512,128]{2,1,0:T(8,128)(2,1)S(1)} collective-permute-done((bf16[4,512,128]{2,1,0:T(8,128)(2,1)S(1)}, bf16[4,512,128]{2,1,0:T(8,128)(2,1)S(1)}, u32[]{:S(2)}, u32[]{:S(2)}) %collective-permute-start.17) | collective-permute-done | bytes 524320 | tf_op jit(solution)/shard_map/ppermute | solution.py:38
  101.9 12.8 %experts.2 = (bf16[256,1152]{1,0:T(8,128)(2,1)}, bf16[256,1152]{1,0:T(8,128)(2,1)}, f32[512,128]{1,0:T(8,128)}, bf16[512,1024]{1,0:T(8,128)(2,1)}, bf16[512,1024]{1,0:T(8,128)(2,1)}, /*index=5*/bf16[512,1024]{1,0:T(8,128)(2,1)}) custom-call(s32[6]{0:T(128)} %stack.24.place_ref._place_ref, bf16[1024,128]{1,0:T(8,128)(2,1)} %pad.39.router_ref, ...), custom_call_target="tpu_custom_call" | custom-call | flops 13799999488 | tf_op jit(solution)/shard_map/experts/pallas_call | solution.py:532
  117.7 12.6 %experts.3 = (bf16[256,1152]{1,0:T(8,128)(2,1)}, bf16[256,1152]{1,0:T(8,128)(2,1)}, f32[512,128]{1,0:T(8,128)}, bf16[512,1024]{1,0:T(8,128)(2,1)}, bf16[512,1024]{1,0:T(8,128)(2,1)}, /*index=5*/bf16[512,1024]{1,0:T(8,128)(2,1)}) custom-call(s32[6]{0:T(128)} %stack.24.place_ref._place_ref, bf16[1024,128]{1,0:T(8,128)(2,1)} %pad.39.router_ref, ...), custom_call_target="tpu_custom_call" | custom-call | flops 13799999488 | tf_op jit(solution)/shard_map/experts/pallas_call | solution.py:532
  136.0 11.9 %grads.1 = (bf16[8,512,128]{2,1,0:T(8,128)(2,1)}, bf16[8,512,128]{2,1,0:T(8,128)(2,1)}, bf16[8,512,128]{2,1,0:T(8,128)(2,1)}, bf16[8,512,128]{2,1,0:T(8,128)(2,1...) custom-call(s32[6]{0:T(128)} %stack.24.place_ref._place_ref, ...), custom_call_target="tpu_custom_call" | custom-call | flops 13799999488 | tf_op jit(solution)/shard_map/grads/pallas_call | solution.py:581
  159.3 6.5 %outputs.1 = (bf16[256,1024]{1,0:T(8,128)(2,1)}, bf16[256,1024]{1,0:T(8,128)(2,1)}, bf16[256,1024]{1,0:T(8,128)(2,1)}, bf16[256,1024]{1,0:T(8,128)(2,1)}) custom-call(s32[6]{0:T(128)} %stack.24.place_ref._place_ref, bf16[8,512,128]{2,1,0:T(8,128)(2,1)} %wd0_ref.1, bf16[512,1024]{1,0:T(8,128)(2,1)} %get-tuple-element.119.refs_0_.refs_8_, ...), custom_call_target="tpu_custom_call" | custom-call | flops 10350000128 | tf_op jit(solution)/shard_map/outputs/pallas_call | solution.py:622
  165.8 3.3 %collective-permute-done.26.refs_2_ = bf16[64,1152]{1,0:T(8,128)(2,1)S(1)} collective-permute-done((bf16[64,1152]{1,0:T(8,128)(2,1)}, bf16[64,1152]{1,0:T(8,128)(2,1)S(1)}, u32[]{:S(2)}, u32[]{:S(2)}) %collective-permute-start.26) | collective-permute-done | bytes 147488 | tf_op jit(solution)/shard_map/ppermute | solution.py:38
  169.8 4.6 %middle_back.1 = (f32[64,1024]{1,0:T(8,128)}, bf16[64,1024]{1,0:T(8,128)(2,1)}, f32[1,1024]{1,0:T(1,128)}, f32[1024,128]{1,0:T(8,128)}, bf16[64,256]{1,0:T(8,128...) custom-call(s32[6]{0:T(128)} %stack.24.place_ref._place_ref, ...), custom_call_target="tpu_custom_call" | custom-call | flops 5175000064 | tf_op jit(solution)/shard_map/middle_back/pallas_call | solution.py:825
  187.2 8.1 %collective-permute-done.31.refs_2_ = bf16[64,1280]{1,0:T(8,128)(2,1)} collective-permute-done((bf16[64,1280]{1,0:T(8,128)(2,1)}, bf16[64,1280]{1,0:T(8,128)(2,1)}, u32[]{:S(2)}, u32[]{:S(2)}) %collective-permute-start.31) | collective-permute-done | bytes 163872 | tf_op jit(solution)/shard_map/ppermute | solution.py:38
  196.1 6.4 %attend_back.1 = (bf16[256,256]{1,0:T(8,128)(2,1)}, bf16[512,256]{1,0:T(8,128)(2,1)}, bf16[512,256]{1,0:T(8,128)(2,1)}) custom-call(s32[6]{0:T(128)} %stack.24.place_ref._place_ref, bf16[256,256]{1,0:T(8,128)(2,1)} %get-tuple-element.135.q_ref, s32[256,1]{1,0:T(8,128)} %copy.64.own_ref, s32[1,1024]{1,0:T(1,128)} %bitcast.56, ...), custom_call_target="tpu_custom_call" | custom-call | flops 6899999744 | tf_op jit(solution)/shard_map/attend_back/pallas_call | solution.py:157
  212.4 3.1 %project_back.1 = (f32[64,1024]{1,0:T(8,128)}, bf16[64,1024]{1,0:T(8,128)(2,1)}, bf16[64,1024]{1,0:T(8,128)(2,1)}, bf16[64,1024]{1,0:T(8,128)(2,1)}, bf16[256,512]{1,0:T(8,128)(2,1)}, /*index=5*/f32[1,1024]{1,0:T(1,128)}) custom-call(s32[6]{0:T(128)} %stack.24.place_ref._place_ref, bf16[256,256]{1,0:T(8,128)(2,1)} %get-tuple-element.146.dq_ref, ...), custom_call_target="tpu_custom_call" | custom-call | flops 3449999872 | tf_op jit(solution)/shard_map/project_back/pallas_call | solution.py:157
  221.2 3.7 %all-to-all-start = ((bf16[4,64,1024]{2,1,0:T(8,128)(2,1)}), bf16[4,64,1024]{2,1,0:T(8,128)(2,1)S(1)}, u32[]{:S(2)}, u32[]{:S(2)}) async-start(bf16[4,64,1024]{2,1,0:T(8,128)(2,1)} %bitcast.23), calls=%async_computation | async-start | bytes 1048576 | tf_op jit(solution)/shard_map/all_to_all | solution.py:860
  224.9 9.5 %collective-permute-done.39 = bf16[64,1024]{1,0:T(8,128)(2,1)S(1)} collective-permute-done((bf16[64,1024]{1,0:T(8,128)(2,1)}, bf16[64,1024]{1,0:T(8,128)(2,1)S(1)}, u32[]{:S(2)}, u32[]{:S(2)}) %collective-permute-start.39) | collective-permute-done | bytes 131104 | tf_op jit(solution)/shard_map/ppermute | solution.py:38
  235.9 3.3 %weights_back.1 = (bf16[512,768]{1,0:T(8,128)(2,1)}, bf16[512,768]{1,0:T(8,128)(2,1)}) custom-call(s32[6]{0:T(128)} %stack.24.place_ref._place_ref, bf16[256,1024]{1,0:T(8,128)(2,1)} %get-tuple-element.158.norm_ref, bf16[256,512]{1,0:T(8,128)(2,1)} %get-tuple-element.160.dlin_ref, bf16[256,256]{1,0:T(8,128)(2,1)} %get-tuple-element.104.refs_0_.att_ref, ...), custom_call_target="tpu_custom_call" | custom-call | flops 3449999872 | tf_op jit(solution)/shard_map/weights_back/pallas_call | solution.py:157
  239.4 4.1 %all-to-all-done = bf16[4,64,1024]{2,1,0:T(8,128)(2,1)S(1)} async-done(((bf16[4,64,1024]{2,1,0:T(8,128)(2,1)}), bf16[4,64,1024]{2,1,0:T(8,128)(2,1)S(1)}, u32[]{:S(2)}, u32[]{:S(2)}) %all-to-all-start) | async-done | bytes 524320 | tf_op jit(solution)/shard_map/all_to_all | solution.py:860
  262.1 4.5 %collective-permute-done.47 = f32[40,128]{1,0:T(8,128)S(1)} collective-permute-done((f32[40,128]{1,0:T(8,128)S(1)}, f32[40,128]{1,0:T(8,128)S(1)}, u32[]{:S(2)}, u32[]{:S(2)}) %collective-permute-start.47) | collective-permute-done | bytes 20512 | tf_op jit(solution)/shard_map/ppermute | solution.py:90
  268.4 5.0 %collective-permute-done.48 = f32[40,128]{1,0:T(8,128)S(1)} collective-permute-done((f32[40,128]{1,0:T(8,128)S(1)}, f32[40,128]{1,0:T(8,128)S(1)}, u32[]{:S(2)}, u32[]{:S(2)}) %collective-permute-start.48) | collective-permute-done | bytes 20512 | tf_op jit(solution)/shard_map/ppermute | solution.py:90
  275.5 3.5 %collective-permute-start.51 = (bf16[128,768]{1,0:T(8,128)(2,1)S(1)}, bf16[128,768]{1,0:T(8,128)(2,1)S(1)}, u32[]{:S(2)}, u32[]{:S(2)}) collective-permute-start(bf16[128,768]{1,0:T(8,128)(2,1)S(1)} %slice.666), channel_id=1, source_target_pairs={{0,16},{16,0},{1,17},{17,1},{2,18},{18,2},{3,19},{19,3},{4,20},{20... | collective-permute-start | bytes 589832 | tf_op jit(solution)/shard_map/ppermute | solution.py:38
  (348 shorter events, 131.2 us)
Async XLA Ops:
  7.2 93.1 %all-gather.3.cloned.1.call-start = ((), (), s32[]{:S(2)}) async-start(), calls=%async_computation.1 | async-start | bytes 3145728 | tf_op jit(solution)/shard_map/all_gather | solution.py:708
  7.9 92.4 %all-gather.5.cloned.1.call-start = ((), (), s32[]{:S(2)}) async-start(), calls=%async_computation.2 | async-start | bytes 3145728 | tf_op jit(solution)/shard_map/all_gather | solution.py:708
  15.7 21.6 %collective-permute-start.4 = (bf16[144,768]{1,0:T(8,128)(2,1)}, bf16[144,768]{1,0:T(8,128)(2,1)S(1)}, u32[]{:S(2)}, u32[]{:S(2)}) collective-permute-start(bf16[144,768]{1,0:T(8,128)(2,1)} %fusion.10.refs_0_), channel_id=1, source_target_pairs={{0,4},{4,0},{8,12},{12,8},{1,5},{5,1},{9,13},{13,9},{2,6},{6,2},{1... | collective-permute-start | bytes 663560 | tf_op jit(solution)/shard_map/ppermute | solution.py:38
  17.1 83.2 %collective-permute-start.16 = (bf16[256,1152]{1,0:T(8,128)(2,1)S(1)}, bf16[256,1152]{1,0:T(8,128)(2,1)}, u32[]{:S(2)}, u32[]{:S(2)}) collective-permute-start(bf16[256,1152]{1,0:T(8,128)(2,1)S(1)} %pad_maximum_fusion.1.refs_2_.refs_4_), channel_id=1, source_target_pairs={{0,4},{4,0},{8,12},{12,8},{1,5},{5,1},{9,13},{13,9},{2,6},{6,2},{1... | collective-permute-start | bytes 1769480 | tf_op jit(solution)/shard_map/ppermute | solution.py:38
  24.5 69.2 %collective-permute-start.21 = (bf16[256,1152]{1,0:T(8,128)(2,1)S(1)}, bf16[256,1152]{1,0:T(8,128)(2,1)}, u32[]{:S(2)}, u32[]{:S(2)}) collective-permute-start(bf16[256,1152]{1,0:T(8,128)(2,1)S(1)} %pad_maximum_fusion.1.refs_2_.refs_4_), channel_id=1, source_target_pairs={{0,8},{4,12},{8,0},{12,4},{1,9},{5,13},{9,1},{13,5},{2,10},{6,14},... | collective-permute-start | bytes 1769480 | tf_op jit(solution)/shard_map/ppermute | solution.py:38
  46.8 26.5 %collective-permute-start.7 = (bf16[1024,256]{1,0:T(8,128)(2,1)S(1)}, bf16[1024,256]{1,0:T(8,128)(2,1)S(1)}, u32[]{:S(2)}, u32[]{:S(2)}) collective-permute-start(bf16[1024,256]{1,0:T(8,128)(2,1)S(1)} %get-tuple-element.264), channel_id=1, source_target_pairs={{0,2},{1,3},{2,0},{3,1},{4,6},{5,7},{6,4},{7,5},{8,10},{9,11},{10,... | collective-permute-start | bytes 1572872 | tf_op jit(solution)/shard_map/ppermute | solution.py:38
  51.7 23.5 %collective-permute-start.5 = (bf16[4,512,128]{2,1,0:T(8,128)(2,1)S(1)}, bf16[4,512,128]{2,1,0:T(8,128)(2,1)}, u32[]{:S(2)}, u32[]{:S(2)}) collective-permute-start(bf16[4,512,128]{2,1,0:T(8,128)(2,1)S(1)} %get-tuple-element.250), channel_id=1, source_target_pairs={{0,16},{16,0},{1,17},{17,1},{2,18},{18,2},{3,19},{19,3},{4,20},{20... | collective-permute-start | bytes 1572872 | tf_op jit(solution)/shard_map/ppermute | solution.py:38
  83.5 16.8 %collective-permute-start.17 = (bf16[4,512,128]{2,1,0:T(8,128)(2,1)S(1)}, bf16[4,512,128]{2,1,0:T(8,128)(2,1)S(1)}, u32[]{:S(2)}, u32[]{:S(2)}) collective-permute-start(bf16[4,512,128]{2,1,0:T(8,128)(2,1)S(1)} %get-tuple-element.249), channel_id=1, source_target_pairs={{0,16},{16,0},{1,17},{17,1},{2,18},{18,2},{3,19},{19,3},{4,20},{20... | collective-permute-start | bytes 1572872 | tf_op jit(solution)/shard_map/ppermute | solution.py:38
  93.7 21.0 %collective-permute-start.22 = (bf16[256,1152]{1,0:T(8,128)(2,1)}, bf16[256,1152]{1,0:T(8,128)(2,1)S(1)}, u32[]{:S(2)}, u32[]{:S(2)}) collective-permute-start(bf16[256,1152]{1,0:T(8,128)(2,1)} %collective-permute-done.21.refs_2_.refs_6_), channel_id=1, source_target_pairs={{0,4},{4,0},{8,12},{12,8},{1,5},{5,1},{9,13},{13,9},{2,6},{6,2},{1... | collective-permute-start | bytes 1769480 | tf_op jit(solution)/shard_map/ppermute | solution.py:38
  94.2 20.4 %collective-permute-start.19 = (bf16[256,1024]{1,0:T(8,128)(2,1)}, bf16[256,1024]{1,0:T(8,128)(2,1)}, u32[]{:S(2)}, u32[]{:S(2)}) collective-permute-start(bf16[256,1024]{1,0:T(8,128)(2,1)} %get-tuple-element.107.refs_0_.norm_ref), channel_id=1, source_target_pairs={{0,8},{4,12},{8,0},{12,4},{1,9},{5,13},{9,1},{13,5},{2,10},{6,14},... | collective-permute-start | bytes 1572872 | tf_op jit(solution)/shard_map/ppermute | solution.py:38
  130.4 19.3 %collective-permute-start.18 = (bf16[256,1152]{1,0:T(8,128)(2,1)S(1)}, bf16[256,1152]{1,0:T(8,128)(2,1)S(1)}, u32[]{:S(2)}, u32[]{:S(2)}) collective-permute-start(bf16[256,1152]{1,0:T(8,128)(2,1)S(1)} %copy-done.31), channel_id=1, source_target_pairs={{0,4},{4,0},{8,12},{12,8},{1,5},{5,1},{9,13},{13,9},{2,6},{6,2},{1... | collective-permute-start | bytes 1769480 | tf_op jit(solution)/shard_map/ppermute | solution.py:38
  135.8 15.6 %collective-permute-start.24 = (bf16[256,1152]{1,0:T(8,128)(2,1)}, bf16[256,1152]{1,0:T(8,128)(2,1)S(1)}, u32[]{:S(2)}, u32[]{:S(2)}) collective-permute-start(bf16[256,1152]{1,0:T(8,128)(2,1)} %fold.4), channel_id=1, source_target_pairs={{0,8},{4,12},{8,0},{12,4},{1,9},{5,13},{9,1},{13,5},{2,10},{6,14},... | collective-permute-start | bytes 1769480 | tf_op jit(solution)/shard_map/ppermute | solution.py:38
  148.0 37.8 %collective-permute-start.28 = (bf16[8,512,128]{2,1,0:T(8,128)(2,1)}, bf16[8,512,128]{2,1,0:T(8,128)(2,1)S(1)}, u32[]{:S(2)}, u32[]{:S(2)}) collective-permute-start(bf16[8,512,128]{2,1,0:T(8,128)(2,1)} %get-tuple-element.130), channel_id=1, source_target_pairs={{0,16},{16,0},{1,17},{17,1},{2,18},{18,2},{3,19},{19,3},{4,20},{20... | collective-permute-start | bytes 3145736 | tf_op jit(solution)/shard_map/ppermute | solution.py:38
  176.1 35.7 %collective-permute-start.33 = (bf16[8,512,128]{2,1,0:T(8,128)(2,1)S(1)}, bf16[8,512,128]{2,1,0:T(8,128)(2,1)}, u32[]{:S(2)}, u32[]{:S(2)}) collective-permute-start(bf16[8,512,128]{2,1,0:T(8,128)(2,1)S(1)} %copy-done.29), channel_id=1, source_target_pairs={{0,16},{16,0},{1,17},{17,1},{2,18},{18,2},{3,19},{19,3},{4,20},{20... | collective-permute-start | bytes 3145736 | tf_op jit(solution)/shard_map/ppermute | solution.py:38
  179.9 15.3 %collective-permute-start.31 = (bf16[64,1280]{1,0:T(8,128)(2,1)}, bf16[64,1280]{1,0:T(8,128)(2,1)}, u32[]{:S(2)}, u32[]{:S(2)}) collective-permute-start(bf16[64,1280]{1,0:T(8,128)(2,1)} %get-tuple-element.139), channel_id=1, source_target_pairs={{0,2},{1,3},{2,0},{3,1},{4,6},{5,7},{6,4},{7,5},{8,10},{9,11},{10,... | collective-permute-start | bytes 491528 | tf_op jit(solution)/shard_map/ppermute | solution.py:38
  185.8 72.9 %collective-permute-start.52 = (bf16[8,512,128]{2,1,0:T(8,128)(2,1)}, bf16[8,512,128]{2,1,0:T(8,128)(2,1)}, u32[]{:S(2)}, u32[]{:S(2)}) collective-permute-start(bf16[8,512,128]{2,1,0:T(8,128)(2,1)} %get-tuple-element.167), channel_id=1, source_target_pairs={{0,16},{16,0},{1,17},{17,1},{2,18},{18,2},{3,19},{19,3},{4,20},{20... | collective-permute-start | bytes 3145736 | tf_op jit(solution)/shard_map/ppermute | solution.py:38
  187.2 20.7 %collective-permute-start.34 = (bf16[256,1024]{1,0:T(8,128)(2,1)S(1)}, bf16[256,1024]{1,0:T(8,128)(2,1)S(1)}, u32[]{:S(2)}, u32[]{:S(2)}) collective-permute-start(bf16[256,1024]{1,0:T(8,128)(2,1)S(1)} %copy-done.35), channel_id=1, source_target_pairs={{0,4},{4,0},{8,12},{12,8},{1,5},{5,1},{9,13},{13,9},{2,6},{6,2},{1... | collective-permute-start | bytes 1572872 | tf_op jit(solution)/shard_map/ppermute | solution.py:38
  218.1 16.4 %collective-permute-start.39 = (bf16[64,1024]{1,0:T(8,128)(2,1)}, bf16[64,1024]{1,0:T(8,128)(2,1)S(1)}, u32[]{:S(2)}, u32[]{:S(2)}) collective-permute-start(bf16[64,1024]{1,0:T(8,128)(2,1)} %get-tuple-element.152), channel_id=1, source_target_pairs={{0,2},{1,3},{2,0},{3,1},{4,6},{5,7},{6,4},{7,5},{8,10},{9,11},{10,... | collective-permute-start | bytes 393224 | tf_op jit(solution)/shard_map/ppermute | solution.py:38
  219.0 15.5 %collective-permute-start.40 = (bf16[64,1024]{1,0:T(8,128)(2,1)}, bf16[64,1024]{1,0:T(8,128)(2,1)S(1)}, u32[]{:S(2)}, u32[]{:S(2)}) collective-permute-start(bf16[64,1024]{1,0:T(8,128)(2,1)} %get-tuple-element.153), channel_id=1, source_target_pairs={{0,3},{1,2},{2,1},{3,0},{4,7},{5,6},{6,5},{7,4},{8,11},{9,10},{10,... | collective-permute-start | bytes 393224 | tf_op jit(solution)/shard_map/ppermute | solution.py:38
  221.2 22.3 %all-to-all-start = ((bf16[4,64,1024]{2,1,0:T(8,128)(2,1)}), bf16[4,64,1024]{2,1,0:T(8,128)(2,1)S(1)}, u32[]{:S(2)}, u32[]{:S(2)}) async-start(bf16[4,64,1024]{2,1,0:T(8,128)(2,1)} %bitcast.23), calls=%async_computation | async-start | bytes 1048576 | tf_op jit(solution)/shard_map/all_to_all | solution.py:860
  239.2 27.5 %collective-permute-start.49 = (bf16[512,768]{1,0:T(8,128)(2,1)}, bf16[512,768]{1,0:T(8,128)(2,1)S(1)}, u32[]{:S(2)}, u32[]{:S(2)}) collective-permute-start(bf16[512,768]{1,0:T(8,128)(2,1)} %get-tuple-element.163), channel_id=1, source_target_pairs={{0,4},{4,0},{8,12},{12,8},{1,5},{5,1},{9,13},{13,9},{2,6},{6,2},{1... | collective-permute-start | bytes 2359304 | tf_op jit(solution)/shard_map/ppermute | solution.py:38
  244.8 29.8 %collective-permute-start.41 = (bf16[64,2048]{1,0:T(8,128)(2,1)S(1)}, bf16[64,2048]{1,0:T(8,128)(2,1)S(1)}, u32[]{:S(2)}, u32[]{:S(2)}) collective-permute-start(bf16[64,2048]{1,0:T(8,128)(2,1)S(1)} %get-tuple-element.262), channel_id=1, source_target_pairs={{0,1},{1,0},{2,3},{3,2},{4,5},{5,4},{6,7},{7,6},{8,9},{9,8},{10,11... | collective-permute-start | bytes 786440 | tf_op jit(solution)/shard_map/ppermute | solution.py:38
  246.3 28.3 %collective-permute-start.42 = (bf16[64,2048]{1,0:T(8,128)(2,1)S(1)}, bf16[64,2048]{1,0:T(8,128)(2,1)S(1)}, u32[]{:S(2)}, u32[]{:S(2)}) collective-permute-start(bf16[64,2048]{1,0:T(8,128)(2,1)S(1)} %get-tuple-element.262), channel_id=1, source_target_pairs={{0,2},{1,3},{2,0},{3,1},{4,6},{5,7},{6,4},{7,5},{8,10},{9,11},{10,... | collective-permute-start | bytes 786440 | tf_op jit(solution)/shard_map/ppermute | solution.py:38
  256.9 17.8 %collective-permute-start.43 = (bf16[64,2048]{1,0:T(8,128)(2,1)S(1)}, bf16[64,2048]{1,0:T(8,128)(2,1)S(1)}, u32[]{:S(2)}, u32[]{:S(2)}) collective-permute-start(bf16[64,2048]{1,0:T(8,128)(2,1)S(1)} %get-tuple-element.262), channel_id=1, source_target_pairs={{0,3},{1,2},{2,1},{3,0},{4,7},{5,6},{6,5},{7,4},{8,11},{9,10},{10,... | collective-permute-start | bytes 786440 | tf_op jit(solution)/shard_map/ppermute | solution.py:38
  (86 other events, 536.6 us)
Sparse Core Ops, SparseCore 0:
  9.6 39.1 all-gather.2
  50.3 41.1 all-gather.4
